TPU v7x, 256 devices: a whole 4x4x8 slice. The times are simulated.
256 devices in a mesh: cols: 32 (over z, y), lev: 8 (over x, core).
Axes of the slice: x: 4, y: 4, z: 8, core: 2. Of those that a mesh axis runs over, the one named last changes fastest.
Arguments:
- departures: float32 [128, 1015808], P('lev', 'cols'), may hold values from -6 to 6
- restrict_offset: int32 [8, 32768], P(None, 'cols'), may hold values from -8192 to 8192, as said below
- restrict_weight: float32 [8, 32768], P(None, 'cols'), may hold values from 0.05 to 0.3
- correlation_count: int32 [32768], P('cols'), may hold values from 1 to 8
- increment: float32 [128, 32768], P('lev', 'cols'), may hold values from -7 to 7
- center: float32 [128, 32768], P('lev', 'cols'), may hold values from 1 to 2
- vertical_coupling: float32 [128, 32768], P('lev', 'cols'), may hold values from -0.4 to 0.4
- neighbors: int32 [4, 32768], P(None, 'cols'), may hold values from 0 to 32767, as said below
- couple: float32 [4, 32768], P(None, 'cols'), may hold values from -0.4 to 0.4
- step_pairs: bfloat16 [4, 128, 32768], P(None, 'lev', 'cols'), may hold values from -13 to 13
- grad_pairs: bfloat16 [4, 128, 32768], P(None, 'lev', 'cols'), may hold values from -30 to 30, as said below
Outputs:
- gradient: float32 [128, 32768], P('lev', 'cols')
- direction: float32 [128, 32768], P('lev', 'cols')
Inputs may be any that keep to these rules, and one draw needn't show every extreme that they name: Entry k of coarse column j's correlation list is the fine column (31 j + restrict_offset[k, j]) modulo 1015808. `neighbors`: rows are the columns j - 1, j + 1, j - a and j + b modulo 32768, with a and b between 1 and 512. grad_pairs is step_pairs times a factor between 0.2 and 2.3 in each entry.
All inputs are finite; a program needn't handle non-finite values.
Results may differ from a plain program's by a relative error of at most 0.0003.
Values sent between devices are 32-bit elements; how exact they have to be, the bound alone decides.
A program may use at most 128 MiB of HBM per device.

v0:
```python
import jax
import jax.numpy as jnp
from jax import lax
from jax.sharding import PartitionSpec as P

K = 8
M = 4
HALO_F = 8192
HALO_C = 512


def padded_2(cells, sides, width, closed):
    for axis, dim in sides:
        count = lax.axis_size(axis)
        ends = count if closed else count - 1
        head = lax.slice_in_dim(cells, 0, width, axis=dim)
        tail = lax.slice_in_dim(cells, cells.shape[dim] - width, cells.shape[dim], axis=dim)
        cells = jnp.concatenate(
            [
                lax.ppermute(tail, axis, [(i, (i + 1) % count) for i in range(ends)]),
                cells,
                lax.ppermute(head, axis, [((i + 1) % count, i) for i in range(ends)]),
            ],
            axis=dim,
        )
    return cells


def passed_along(value, axis, steps):
    count = lax.axis_size(axis)
    pairs = [(source, (source + steps) % count) for source in range(count)]
    return lax.ppermute(value, axis, pairs)


def vertical_term(column_field, vertical_coupling):
    stacked = jnp.stack([column_field, vertical_coupling])
    padded = padded_2(stacked, (("lev", 1),), 1, False)
    values_ext = padded[0]
    coupling_ext = padded[1]
    return coupling_ext[1:-1] * values_ext[2:] + coupling_ext[:-2] * values_ext[:-2]


def per_device(
    departures,
    restrict_offset,
    restrict_weight,
    correlation_count,
    increment,
    center,
    vertical_coupling,
    neighbors,
    couple,
    step_pairs,
    grad_pairs,
):
    tile = lax.axis_index("cols")
    tiles = lax.axis_size("cols")
    fine_cols = departures.shape[1]
    coarse_cols = increment.shape[1]
    spacing = fine_cols // coarse_cols
    coarse_total = coarse_cols * tiles
    entries = jnp.arange(K, dtype=jnp.int32)[:, None]
    live_weight = jnp.where(entries < correlation_count[None, :], restrict_weight, jnp.float32(0.0))
    extended = padded_2(departures, (("cols", 1),), HALO_F, True)
    local_columns = jnp.arange(coarse_cols, dtype=jnp.int32)[None, :]
    local_index = spacing * local_columns + restrict_offset + HALO_F
    restricted = jnp.zeros(increment.shape, jnp.float32)
    for entry in range(K):
        restricted = restricted + live_weight[entry][None, :] * jnp.take(
            extended, local_index[entry], axis=1
        )
    coarse_ext = padded_2(increment, (("cols", 1),), HALO_C, True)
    neighbor_local = (neighbors - tile * coarse_cols + HALO_C) % coarse_total
    image = center * increment + vertical_term(increment, vertical_coupling)
    for side in range(4):
        image = image + couple[side][None, :] * jnp.take(coarse_ext, neighbor_local[side], axis=1)
    misfit = image - restricted
    spread_back = jnp.zeros((increment.shape[0], coarse_cols + 2 * HALO_C), jnp.float32)
    for side in range(4):
        spread_back = spread_back.at[:, neighbor_local[side]].add(couple[side][None, :] * misfit)
    low_rim = spread_back[:, :HALO_C]
    high_rim = spread_back[:, coarse_cols + HALO_C :]
    middle = spread_back[:, HALO_C : coarse_cols + HALO_C]
    from_above = passed_along(low_rim, "cols", -1)
    from_below = passed_along(high_rim, "cols", 1)
    middle = middle.at[:, :HALO_C].add(from_below)
    middle = middle.at[:, coarse_cols - HALO_C :].add(from_above)
    adjoint = center * misfit + vertical_term(misfit, vertical_coupling) + middle
    gradient = increment + adjoint
    local_curv = jnp.stack(
        [
            jnp.sum(step_pairs[pair].astype(jnp.float32) * grad_pairs[pair].astype(jnp.float32))
            for pair in range(M)
        ]
    )
    last_grad = grad_pairs[M - 1].astype(jnp.float32)
    curvatures, last_norm = lax.psum((local_curv, jnp.sum(last_grad * last_grad)), ("cols", "lev"))
    inverses = 1.0 / curvatures

    def inner_product(first, second):
        return lax.psum(jnp.sum(first * second), ("cols", "lev"))

    current = gradient
    alphas = [None] * M
    for pair in range(M - 1, -1, -1):
        alphas[pair] = inverses[pair] * inner_product(step_pairs[pair].astype(jnp.float32), current)
        current = current - alphas[pair] * grad_pairs[pair].astype(jnp.float32)
    current = curvatures[M - 1] / last_norm * current
    for pair in range(M):
        betas = inverses[pair] * inner_product(grad_pairs[pair].astype(jnp.float32), current)
        current = current + (alphas[pair] - betas) * step_pairs[pair].astype(jnp.float32)
    return (gradient, -current)


def solution(mesh):
    return jax.shard_map(
        per_device,
        mesh=mesh,
        in_specs=(
            P("lev", "cols"),
            P(None, "cols"),
            P(None, "cols"),
            P("cols"),
            P("lev", "cols"),
            P("lev", "cols"),
            P("lev", "cols"),
            P(None, "cols"),
            P(None, "cols"),
            P(None, "lev", "cols"),
            P(None, "lev", "cols"),
        ),
        out_specs=(P("lev", "cols"), P("lev", "cols")),
        check_vma=False,
    )
```

profile of v0, /device:TPU:8, one launch (start us, length us, event | category | flops | bytes accessed | tf_op | source)
XLA Modules:
  0.0 874.2 jit_solution(11981496509512834402)
XLA Ops:
  3.4 1.7 collective-permute-start.1
  5.2 2.3 fusion.85
  7.5 1.6 collective-permute-start.4
  11.9 1.6 collective-permute-start.2
  33.7 1.9 copy.165
  37.3 5.2 collective-permute-start.3
  47.7 4.3 gather_fusion
  52.0 4.3 gather_fusion.1
  56.3 4.3 gather_fusion.2
  60.7 4.3 gather_fusion.3
  65.0 3.8 pad_maximum_fusion
  68.8 12.7 %copy.157 = f32[16,48128]{0,1:T(8,128)} copy(f32[16,48128]{1,0:T(8,128)} %pad_maximum_fusion) | data formatting | bytes 6160384 | tf_op jit(solution)/shard_map/concatenate | solution.py:18
  81.5 12.0 %gather_fusion.4 = f32[1024,16]{1,0:T(8,128)} fusion(f32[16,48128]{0,1:T(8,128)} %copy.157, s32[1024]{0:T(1024)S(1)} %copy-done.18), kind=kCustom, calls=%fused_computation.1.clone | custom fusion | bytes 135168 | tf_op jit(solution)/shard_map/jit(_take)/gather | solution.py:69
  93.6 12.0 %gather_fusion.5 = f32[1024,16]{1,0:T(8,128)} fusion(f32[16,48128]{0,1:T(8,128)} %copy.157, s32[1024]{0:T(1024)S(1)} %copy-done.19), kind=kCustom, calls=%fused_computation.5.clone | custom fusion | bytes 135168 | tf_op jit(solution)/shard_map/jit(_take)/gather | solution.py:69
  105.6 12.0 %gather_fusion.6 = f32[1024,16]{1,0:T(8,128)} fusion(f32[16,48128]{0,1:T(8,128)} %copy.157, s32[1024]{0:T(1024)S(1)} %copy-done.17), kind=kCustom, calls=%fused_computation.6.clone | custom fusion | bytes 135168 | tf_op jit(solution)/shard_map/jit(_take)/gather | solution.py:69
  117.5 12.0 %gather_fusion.7 = f32[1024,16]{1,0:T(8,128)} fusion(f32[16,48128]{0,1:T(8,128)} %copy.157, s32[1024]{0:T(1024)S(1)} %copy-done.16), kind=kCustom, calls=%fused_computation.7.clone | custom fusion | bytes 135168 | tf_op jit(solution)/shard_map/jit(_take)/gather | solution.py:69
  129.5 12.0 %gather_fusion.8 = f32[1024,16]{1,0:T(8,128)} fusion(f32[16,48128]{0,1:T(8,128)} %copy.157, s32[1024]{0:T(1024)S(1)} %copy-done.15), kind=kCustom, calls=%fused_computation.8.clone | custom fusion | bytes 135168 | tf_op jit(solution)/shard_map/jit(_take)/gather | solution.py:69
  141.5 12.0 %gather_fusion.9 = f32[1024,16]{1,0:T(8,128)} fusion(f32[16,48128]{0,1:T(8,128)} %copy.157, s32[1024]{0:T(1024)S(1)} %copy-done.14), kind=kCustom, calls=%fused_computation.9.clone | custom fusion | bytes 135168 | tf_op jit(solution)/shard_map/jit(_take)/gather | solution.py:69
  153.5 12.0 %gather_fusion.10 = f32[1024,16]{1,0:T(8,128)} fusion(f32[16,48128]{0,1:T(8,128)} %copy.157, s32[1024]{0:T(1024)S(1)} %copy-done.13), kind=kCustom, calls=%fused_computation.10.clone | custom fusion | bytes 135168 | tf_op jit(solution)/shard_map/jit(_take)/gather | solution.py:69
  165.5 12.0 %gather_fusion.11 = f32[1024,16]{1,0:T(8,128)} fusion(f32[16,48128]{0,1:T(8,128)} %copy.157, s32[1024]{0:T(1024)S(1)} %copy-done.12), kind=kCustom, calls=%fused_computation.11.clone | custom fusion | bytes 135168 | tf_op jit(solution)/shard_map/jit(_take)/gather | solution.py:69
  177.7 7.8 fusion.39
  185.5 1.7 slice_maximum_fusion
  187.2 1.6 copy.169
  188.8 3.9 collective-permute-start.7
  192.7 7.7 scatter_custom_fusion
  200.4 8.3 scatter_custom_fusion.1
  208.7 8.3 scatter_custom_fusion.2
  216.9 8.3 scatter_custom_fusion.3
  225.2 1.8 fusion.86
  227.0 1.9 slice.374
  228.8 5.0 collective-permute-start.9
  238.4 2.6 fusion.1
  242.3 2.5 fusion.62
  244.8 1.7 fusion.63
  246.5 2.8 fusion.2
  249.3 2.6 pad_maximum_fusion.10
  251.8 80.1 %all-reduce.1 = (f32[4]{0:T(128)S(1)}, f32[]{:T(128)}) all-reduce(f32[4]{0:T(128)S(1)} %pad_maximum_fusion.10, f32[]{:T(128)} %get-tuple-element.40), channel_id=1, replica_groups=mesh['cols'=32,'lev'=8] {'cols','lev'}, use_global_device_ids=true, to_apply=%region_9.12 | all-reduce | flops 5 | bytes 40 | tf_op jit(solution)/shard_map/psum | solution.py:97
  335.4 74.6 %psum.73 = f32[]{:T(128)} all-reduce(f32[]{:T(128)} %get-tuple-element.39), channel_id=1, replica_groups=mesh['cols'=32,'lev'=8] {'cols','lev'}, use_global_device_ids=true, to_apply=%region_15.18 | all-reduce | flops 1 | bytes 8 | tf_op jit(solution)/shard_map/psum | solution.py:101
  411.3 1.8 fusion.10
  413.1 73.3 %psum.74 = f32[]{:T(128)} all-reduce(f32[]{:T(128)} %get-tuple-element.48), channel_id=1, replica_groups=mesh['cols'=32,'lev'=8] {'cols','lev'}, use_global_device_ids=true, to_apply=%region_17.20 | all-reduce | flops 1 | bytes 8 | tf_op jit(solution)/shard_map/psum | solution.py:101
  488.4 74.3 %all-reduce = (f32[]{:T(128)}, f32[]{:T(128)}) all-reduce(f32[]{:T(128)} %fusion.15, f32[]{:T(128)} %get-tuple-element.38), channel_id=1, replica_groups=mesh['cols'=32,'lev'=8] {'cols','lev'}, use_global_device_ids=true, to_apply=%region_19.22 | all-reduce | flops 2 | bytes 16 | tf_op jit(solution)/shard_map/psum | solution.py:101
  565.2 1.7 fusion.20
  567.0 73.4 %psum.76 = f32[]{:T(128)} all-reduce(f32[]{:T(128)} %fusion.20), channel_id=1, replica_groups=mesh['cols'=32,'lev'=8] {'cols','lev'}, use_global_device_ids=true, to_apply=%region_21.24 | all-reduce | flops 1 | bytes 8 | tf_op jit(solution)/shard_map/psum | solution.py:101
  641.6 1.8 fusion.14
  643.4 74.2 %psum.77 = f32[]{:T(128)} all-reduce(f32[]{:T(128)} %get-tuple-element.46), channel_id=1, replica_groups=mesh['cols'=32,'lev'=8] {'cols','lev'}, use_global_device_ids=true, to_apply=%region_23.26 | all-reduce | flops 1 | bytes 8 | tf_op jit(solution)/shard_map/psum | solution.py:101
  718.9 1.7 fusion.9
  720.6 73.3 %psum.78 = f32[]{:T(128)} all-reduce(f32[]{:T(128)} %fusion.9), channel_id=1, replica_groups=mesh['cols'=32,'lev'=8] {'cols','lev'}, use_global_device_ids=true, to_apply=%region_25.28 | all-reduce | flops 1 | bytes 8 | tf_op jit(solution)/shard_map/psum | solution.py:101
  796.9 74.2 %psum.79 = f32[]{:T(128)} all-reduce(f32[]{:T(128)} %fusion.24), channel_id=1, replica_groups=mesh['cols'=32,'lev'=8] {'cols','lev'}, use_global_device_ids=true, to_apply=%region_27.30 | all-reduce | flops 1 | bytes 8 | tf_op jit(solution)/shard_map/psum | solution.py:101
  (142 shorter events, 44.8 us)
Async XLA Ops:
  3.4 33.9 %collective-permute-start.1 = (f32[2,1,1024]{2,0,1:T(2,128)S(1)}, f32[2,1,1024]{2,0,1:T(2,128)S(1)}, u32[]{:S(2)}, u32[]{:S(2)}) collective-permute-start(f32[2,1,1024]{2,0,1:T(2,128)S(1)} %copy.151), channel_id=1, source_target_pairs={{0,1},{1,2},{2,3},{3,4},{4,5},{5,6},{6,7},{8,9},{9,10},{10,11},{11... | collective-permute-start | bytes 24584 | tf_op jit(solution)/shard_map/ppermute | solution.py:20
  7.5 57.5 %collective-permute-start.4 = (f32[16,8192]{1,0:T(8,128)}, f32[16,8192]{1,0:T(8,128)}, u32[]{:S(2)}, u32[]{:S(2)}) collective-permute-start(f32[16,8192]{1,0:T(8,128)} %get-tuple-element.51), channel_id=1, source_target_pairs={{0,8},{8,16},{16,24},{24,32},{32,40},{40,48},{48,56},{56,64},{64,7... | collective-permute-start | bytes 1572872 | tf_op jit(solution)/shard_map/ppermute | solution.py:20
  9.0 56.0 %collective-permute-start.5 = (f32[16,8192]{1,0:T(8,128)}, f32[16,8192]{1,0:T(8,128)}, u32[]{:S(2)}, u32[]{:S(2)}) collective-permute-start(f32[16,8192]{1,0:T(8,128)} %get-tuple-element.52), channel_id=1, source_target_pairs={{8,0},{16,8},{24,16},{32,24},{40,32},{48,40},{56,48},{64,56},{72,6... | collective-permute-start | bytes 1572872 | tf_op jit(solution)/shard_map/ppermute | solution.py:22
  9.8 34.4 %collective-permute-start = (f32[2,1,1024]{2,0,1:T(2,128)S(1)}, f32[2,1,1024]{2,0,1:T(2,128)S(1)}, u32[]{:S(2)}, u32[]{:S(2)}) collective-permute-start(f32[2,1,1024]{2,0,1:T(2,128)S(1)} %copy.148), channel_id=1, source_target_pairs={{1,0},{2,1},{3,2},{4,3},{5,4},{6,5},{7,6},{9,8},{10,9},{11,10},{12... | collective-permute-start | bytes 24584 | tf_op jit(solution)/shard_map/ppermute | solution.py:22
  11.9 33.7 %collective-permute-start.2 = (f32[16,512]{1,0:T(8,128)S(1)}, f32[16,512]{1,0:T(8,128)S(1)}, u32[]{:S(2)}, u32[]{:S(2)}) collective-permute-start(f32[16,512]{1,0:T(8,128)S(1)} %get-tuple-element.67), channel_id=1, source_target_pairs={{0,8},{8,16},{16,24},{24,32},{32,40},{40,48},{48,56},{56,64},{64,7... | collective-permute-start | bytes 98312 | tf_op jit(solution)/shard_map/ppermute | solution.py:20
  31.0 1.7 copy-start.2
  32.9 2.7 copy-start.1
  37.3 8.9 %collective-permute-start.3 = (f32[16,512]{1,0:T(8,128)S(1)}, f32[16,512]{1,0:T(8,128)}, u32[]{:S(2)}, u32[]{:S(2)}) collective-permute-start(f32[16,512]{1,0:T(8,128)S(1)} %get-tuple-element.68), channel_id=1, source_target_pairs={{8,0},{16,8},{24,16},{32,24},{40,32},{48,40},{56,48},{64,56},{72,6... | collective-permute-start | bytes 98312 | tf_op jit(solution)/shard_map/ppermute | solution.py:22
  45.6 0.6 copy-start.3
  47.4 34.1 %copy-start.18 = (s32[1024]{0:T(1024)S(1)}, s32[1024]{0:T(1024)}, u32[]{:S(2)}) copy-start(s32[1024]{0:T(1024)} %fusion.74) | copy-start | bytes 12292
  47.4 46.1 %copy-start.19 = (s32[1024]{0:T(1024)S(1)}, s32[1024]{0:T(1024)}, u32[]{:S(2)}) copy-start(s32[1024]{0:T(1024)} %fusion.75) | copy-start | bytes 12292
  47.4 58.1 %copy-start.17 = (s32[1024]{0:T(1024)S(1)}, s32[1024]{0:T(1024)}, u32[]{:S(2)}) copy-start(s32[1024]{0:T(1024)} %fusion.76) | copy-start | bytes 12292
  47.4 70.1 %copy-start.16 = (s32[1024]{0:T(1024)S(1)}, s32[1024]{0:T(1024)}, u32[]{:S(2)}) copy-start(s32[1024]{0:T(1024)} %fusion.77) | copy-start | bytes 12292
  47.4 82.1 %copy-start.15 = (s32[1024]{0:T(1024)S(1)}, s32[1024]{0:T(1024)}, u32[]{:S(2)}) copy-start(s32[1024]{0:T(1024)} %fusion.78) | copy-start | bytes 12292
  47.4 94.1 %copy-start.14 = (s32[1024]{0:T(1024)S(1)}, s32[1024]{0:T(1024)}, u32[]{:S(2)}) copy-start(s32[1024]{0:T(1024)} %fusion.79) | copy-start | bytes 12292
  47.5 106.1 %copy-start.13 = (s32[1024]{0:T(1024)S(1)}, s32[1024]{0:T(1024)}, u32[]{:S(2)}) copy-start(s32[1024]{0:T(1024)} %fusion.80) | copy-start | bytes 12292
  47.5 118.1 %copy-start.12 = (s32[1024]{0:T(1024)S(1)}, s32[1024]{0:T(1024)}, u32[]{:S(2)}) copy-start(s32[1024]{0:T(1024)} %fusion.81) | copy-start | bytes 12292
  47.5 130.0 %copy-start.4 = (f32[1,1024]{1,0:T(1,128)S(1)}, f32[1,1024]{1,0:T(1,128)}, u32[]{:S(2)}) copy-start(f32[1,1024]{1,0:T(1,128)} %get-tuple-element.69) | copy-start | bytes 12292
  47.5 130.0 %copy-start.5 = (f32[1,1024]{1,0:T(1,128)S(1)}, f32[1,1024]{1,0:T(1,128)}, u32[]{:S(2)}) copy-start(f32[1,1024]{1,0:T(1,128)} %get-tuple-element.70) | copy-start | bytes 12292
  47.5 130.0 %copy-start.6 = (f32[1,1024]{1,0:T(1,128)S(1)}, f32[1,1024]{1,0:T(1,128)}, u32[]{:S(2)}) copy-start(f32[1,1024]{1,0:T(1,128)} %get-tuple-element.71) | copy-start | bytes 12292
  47.5 130.0 %copy-start.7 = (f32[1,1024]{1,0:T(1,128)S(1)}, f32[1,1024]{1,0:T(1,128)}, u32[]{:S(2)}) copy-start(f32[1,1024]{1,0:T(1,128)} %get-tuple-element.72) | copy-start | bytes 12292
  47.5 130.0 %copy-start.8 = (f32[1,1024]{1,0:T(1,128)S(1)}, f32[1,1024]{1,0:T(1,128)}, u32[]{:S(2)}) copy-start(f32[1,1024]{1,0:T(1,128)} %get-tuple-element.73) | copy-start | bytes 12292
  47.5 130.0 %copy-start.9 = (f32[1,1024]{1,0:T(1,128)S(1)}, f32[1,1024]{1,0:T(1,128)}, u32[]{:S(2)}) copy-start(f32[1,1024]{1,0:T(1,128)} %get-tuple-element.74) | copy-start | bytes 12292
  47.5 130.0 %copy-start.10 = (f32[1,1024]{1,0:T(1,128)S(1)}, f32[1,1024]{1,0:T(1,128)}, u32[]{:S(2)}) copy-start(f32[1,1024]{1,0:T(1,128)} %get-tuple-element.75) | copy-start | bytes 12292
  47.5 130.0 %copy-start.11 = (f32[1,1024]{1,0:T(1,128)S(1)}, f32[1,1024]{1,0:T(1,128)}, u32[]{:S(2)}) copy-start(f32[1,1024]{1,0:T(1,128)} %get-tuple-element.76) | copy-start | bytes 12292
  47.6 130.0 %copy-start.20 = (pred[1024]{0:T(1024)(128)(4,1)S(1)}, pred[1024]{0:T(1024)(128)(4,1)}, u32[]{:S(2)}) copy-start(pred[1024]{0:T(1024)(128)(4,1)} %get-tuple-element.101) | copy-start | bytes 3076
  47.6 130.0 %copy-start.21 = (pred[1024]{0:T(1024)(128)(4,1)S(1)}, pred[1024]{0:T(1024)(128)(4,1)}, u32[]{:S(2)}) copy-start(pred[1024]{0:T(1024)(128)(4,1)} %get-tuple-element.102) | copy-start | bytes 3076
  47.6 130.0 %copy-start.22 = (pred[1024]{0:T(1024)(128)(4,1)S(1)}, pred[1024]{0:T(1024)(128)(4,1)}, u32[]{:S(2)}) copy-start(pred[1024]{0:T(1024)(128)(4,1)} %get-tuple-element.103) | copy-start | bytes 3076
  47.6 130.0 %copy-start.23 = (pred[1024]{0:T(1024)(128)(4,1)S(1)}, pred[1024]{0:T(1024)(128)(4,1)}, u32[]{:S(2)}) copy-start(pred[1024]{0:T(1024)(128)(4,1)} %get-tuple-element.104) | copy-start | bytes 3076
  47.6 130.0 %copy-start.24 = (pred[1024]{0:T(1024)(128)(4,1)S(1)}, pred[1024]{0:T(1024)(128)(4,1)}, u32[]{:S(2)}) copy-start(pred[1024]{0:T(1024)(128)(4,1)} %get-tuple-element.105) | copy-start | bytes 3076
  47.6 130.0 %copy-start.25 = (pred[1024]{0:T(1024)(128)(4,1)S(1)}, pred[1024]{0:T(1024)(128)(4,1)}, u32[]{:S(2)}) copy-start(pred[1024]{0:T(1024)(128)(4,1)} %get-tuple-element.106) | copy-start | bytes 3076
  47.6 130.0 %copy-start.26 = (pred[1024]{0:T(1024)(128)(4,1)S(1)}, pred[1024]{0:T(1024)(128)(4,1)}, u32[]{:S(2)}) copy-start(pred[1024]{0:T(1024)(128)(4,1)} %get-tuple-element.107) | copy-start | bytes 3076
  47.6 130.0 %copy-start.27 = (pred[1024]{0:T(1024)(128)(4,1)S(1)}, pred[1024]{0:T(1024)(128)(4,1)}, u32[]{:S(2)}) copy-start(pred[1024]{0:T(1024)(128)(4,1)} %get-tuple-element.108) | copy-start | bytes 3076
  47.6 130.0 %copy-start.28 = (pred[1024]{0:T(1024)(128)(4,1)S(1)}, pred[1024]{0:T(1024)(128)(4,1)}, u32[]{:S(2)}) copy-start(pred[1024]{0:T(1024)(128)(4,1)} %get-tuple-element.111) | copy-start | bytes 3076
  47.6 130.0 %copy-start.29 = (pred[1024]{0:T(1024)(128)(4,1)S(1)}, pred[1024]{0:T(1024)(128)(4,1)}, u32[]{:S(2)}) copy-start(pred[1024]{0:T(1024)(128)(4,1)} %get-tuple-element.112) | copy-start | bytes 3076
  47.7 130.0 %copy-start.30 = (pred[1024]{0:T(1024)(128)(4,1)S(1)}, pred[1024]{0:T(1024)(128)(4,1)}, u32[]{:S(2)}) copy-start(pred[1024]{0:T(1024)(128)(4,1)} %get-tuple-element.109) | copy-start | bytes 3076
  47.7 130.0 %copy-start.31 = (pred[1024]{0:T(1024)(128)(4,1)S(1)}, pred[1024]{0:T(1024)(128)(4,1)}, u32[]{:S(2)}) copy-start(pred[1024]{0:T(1024)(128)(4,1)} %get-tuple-element.110) | copy-start | bytes 3076
  65.0 112.7 %copy-start = (f32[16,1024]{0,1:T(8,128)S(1)}, f32[16,1024]{0,1:T(8,128)}, u32[]{:S(2)}) copy-start(f32[16,1024]{0,1:T(8,128)} %copy.165) | copy-start | bytes 196612
  188.8 48.2 %collective-permute-start.7 = (f32[2,1,1024]{2,0,1:T(2,128)S(1)}, f32[2,1,1024]{2,0,1:T(2,128)S(1)}, u32[]{:S(2)}, u32[]{:S(2)}) collective-permute-start(f32[2,1,1024]{2,0,1:T(2,128)S(1)} %copy.169), channel_id=1, source_target_pairs={{0,1},{1,2},{2,3},{3,4},{4,5},{5,6},{6,7},{8,9},{9,10},{10,11},{11... | collective-permute-start | bytes 24584 | tf_op jit(solution)/shard_map/ppermute | solution.py:20
  228.8 13.5 %collective-permute-start.8 = (f32[16,512]{0,1:T(8,128)}, f32[16,512]{0,1:T(8,128)}, u32[]{:S(2)}, u32[]{:S(2)}) collective-permute-start(f32[16,512]{0,1:T(8,128)} %get-tuple-element.56), channel_id=1, source_target_pairs={{0,8},{8,16},{16,24},{24,32},{32,40},{40,48},{48,56},{56,64},{64,7... | collective-permute-start | bytes 98312 | tf_op jit(solution)/shard_map/ppermute | solution.py:32
  228.8 16.0 %collective-permute-start.9 = (f32[16,512]{0,1:T(8,128)S(1)}, f32[16,512]{0,1:T(8,128)S(1)}, u32[]{:S(2)}, u32[]{:S(2)}) collective-permute-start(f32[16,512]{0,1:T(8,128)S(1)} %get-tuple-element.55), channel_id=1, source_target_pairs={{0,248},{8,0},{16,8},{24,16},{32,24},{40,32},{48,40},{56,48},{64,5... | collective-permute-start | bytes 98312 | tf_op jit(solution)/shard_map/ppermute | solution.py:32
  235.4 5.5 collective-permute-start.6
where the time goes:
time: 879 us; the launch traced here: 874 us
  blocking collectives  597 us (68%)
  local copies, waits for them, and re-layouts  154 us (18%)
  other arithmetic  87.4 us (10%)
  starting transfers between devices  22.3 us (3%)
  between operations  12.8 us (1%)
    psum x7, blocking collectives, inner_product(): return lax.psum(jnp.sum(first * second), ('cols', 'lev'))  517 us
    gather x8, local copies, waits for them, and re-layouts, per_device(): jnp.take(extended, local_index[entry], axis=1)  95.9 us
    psum x1, blocking collectives, per_device(): lax.psum((local_curv, jnp.sum(last_grad * last_grad)), ('cols', 'lev'))  80.1 us
    scatter-add x4, other arithmetic, per_device(): spread_back.at[:, neighbor_local[side]].add(couple[side][None, :] * misfit)  32.5 us
  transfers between devices with their start and end apart: 10, of which 0 were waited for; matrix products, arithmetic and copies ran while one was open for 11% of the time, Pallas kernels for 0%

commit v1 on v0

v1 whole, which is shorter than its diff:
```python
import functools

import jax
import jax.numpy as jnp
from jax import lax
from jax.experimental import pallas as pl
from jax.experimental.pallas import tpu as pltpu
from jax.sharding import PartitionSpec as P

K = 8
M = 4
RATIO = 31
ROWS = 16
COLS = 1024
FINE = RATIO * COLS
SEG = 4096
HALO = 512
EXT = COLS + 2 * HALO
EDGE = 384
OWN = COLS // 128
FOREIGN = 2 * EDGE // 128
UNROLL = 16
WIDE = 256
REACH = WIDE + HALO
NY = 4
F32 = jnp.float32
I32 = jnp.int32
BF16 = jnp.bfloat16


def halves(value):
    high = value.astype(BF16)
    low = (value - high.astype(F32)).astype(BF16)
    return jnp.concatenate([high, low], axis=0)


def lane_sums(value):
    total = value[0:8] + value[8:16]
    parts = [total[:, 128 * i : 128 * i + 128] for i in range(COLS // 128)]
    while len(parts) > 1:
        parts = [parts[i] + parts[i + 1] for i in range(0, len(parts), 2)]
    return jnp.sum(parts[0], axis=0, keepdims=True)


def kernel(
    tiles,
    slabs,
    dep_hbm,
    off_hbm,
    wgt_hbm,
    cnt_hbm,
    inc_hbm,
    cen_hbm,
    vc_hbm,
    nbr_hbm,
    cpl_hbm,
    step_hbm,
    grad_hbm,
    gradient_ref,
    direction_ref,
    dep,
    off,
    wgt,
    cnt,
    cen,
    vc,
    nbr,
    cpl,
    steps,
    grads,
    fine,
    table,
    acc,
    f_own,
    w_own,
    r_own,
    f_out,
    w_out,
    f_for,
    w_for,
    r_for,
    idx_own,
    idx_for,
    inc,
    parts,
    onehot,
    up_out,
    below,
    down_out,
    above,
    sum_out,
    sum_in,
    restricted,
    mis_out,
    mis_in,
    spread,
    rim_in,
    prods,
    red_lev,
    red_y,
    red_z,
    local_sem,
    send_sem,
    recv_sem,
    lev_send,
    lev_recv,
    y_send,
    y_recv,
    z_send,
    z_recv,
):
    tile = lax.axis_index("cols")
    slab = lax.axis_index("lev")
    nz = tiles // NY
    row_z = tile // NY
    row_y = lax.rem(tile, NY)
    left = lax.rem(tile + tiles - 1, tiles)
    right = lax.rem(tile + 1, tiles)
    lower = lax.rem(slab + slabs - 1, slabs)
    upper = lax.rem(slab + 1, slabs)

    def spot(column, level):
        return {"cols": column, "lev": level}

    lev_peers = [spot(tile, lax.rem(slab + d, slabs)) for d in range(1, slabs)]
    y_peers = [spot(row_z * NY + lax.rem(row_y + d, NY), slab) for d in range(1, NY)]
    z_peers = [spot(lax.rem(row_z + d, nz) * NY + row_y, slab) for d in range(1, nz)]

    def send(src, dst, i, target):
        copy = pltpu.make_async_remote_copy(
            src_ref=src,
            dst_ref=dst,
            send_sem=send_sem.at[i],
            recv_sem=recv_sem.at[i],
            device_id=target,
            device_id_type=pl.DeviceIdType.MESH,
        )
        copy.start()
        return copy

    loads = []
    for i, (src, dst) in enumerate(
        [
            (off_hbm, off),
            (wgt_hbm, wgt),
            (cnt_hbm, cnt),
            (inc_hbm, inc.at[:, HALO : HALO + COLS]),
            (vc_hbm, vc),
            (dep_hbm, dep),
            (nbr_hbm, nbr),
            (cpl_hbm, cpl),
            (cen_hbm, cen),
            (step_hbm, steps),
            (grad_hbm, grads),
        ]
    ):
        copy = pltpu.make_async_copy(src, dst, local_sem.at[i])
        copy.start()
        loads.append(copy)

    barrier = pltpu.get_barrier_semaphore()
    greeted = lev_peers + y_peers + z_peers + [spot(left, slab), spot(right, slab)]
    for peer in greeted:
        pl.semaphore_signal(barrier, inc=1, device_id=peer, device_id_type=pl.DeviceIdType.MESH)

    for i in range(5):
        loads[i].wait()

    lane = lax.broadcasted_iota(I32, (8, 128), 1)
    entry = lax.broadcasted_iota(I32, (8, 128), 0)
    for b in range(OWN):
        cut = slice(128 * b, 128 * b + 128)
        f = RATIO * (128 * b + lane) + off[:, cut]
        w = jnp.where(entry < cnt[:, cut], wgt[:, cut], 0.0)
        here = (f >= 0) & (f < FINE)
        fo = jnp.where(here, f, 0)
        f_own[b] = fo
        r_own[b] = fo & (SEG - 1)
        w_own[b] = jnp.where(here, w, 0.0)
        if b < FOREIGN // 2:
            f_out[b] = jnp.where(f < 0, f + FINE, 0)
            w_out[b] = jnp.where(f < 0, w, 0.0)
        if b >= OWN - FOREIGN // 2:
            at = b - OWN + FOREIGN
            f_out[at] = jnp.where(f >= FINE, f - FINE, 0)
            w_out[at] = jnp.where(f >= FINE, w, 0.0)
    own_index = pltpu.make_async_copy(r_own, idx_own, local_sem.at[11])
    own_index.start()
    up_out[0:1, :] = inc[ROWS - 1 : ROWS, HALO : HALO + COLS]
    up_out[1:2, :] = vc[ROWS - 1 : ROWS, :]
    down_out[...] = inc[0:1, HALO : HALO + COLS]

    pl.semaphore_wait(barrier, len(greeted))

    half = FOREIGN // 2
    to_left, to_right = spot(left, slab), spot(right, slab)
    to_lower, to_upper = spot(tile, lower), spot(tile, upper)
    lists = [
        send(f_out.at[0:half], f_for.at[0:half], 0, to_left),
        send(w_out.at[0:half], w_for.at[0:half], 1, to_left),
        send(f_out.at[half:FOREIGN], f_for.at[half:FOREIGN], 2, to_right),
        send(w_out.at[half:FOREIGN], w_for.at[half:FOREIGN], 3, to_right),
    ]
    halos = [
        send(inc.at[:, HALO : 2 * HALO], inc.at[:, HALO + COLS : EXT], 4, to_left),
        send(inc.at[:, COLS : COLS + HALO], inc.at[:, 0:HALO], 5, to_right),
        send(up_out, below, 6, to_upper),
        send(down_out, above, 7, to_lower),
    ]

    loads[5].wait()
    last = FINE // SEG
    tail = FINE - last * SEG
    for b in range(SEG // 128):
        pieces = [dep[:, SEG * g + 128 * b : SEG * g + 128 * b + 128] for g in range(last)]
        if 128 * b < tail:
            pieces.append(dep[:, SEG * last + 128 * b : SEG * last + 128 * b + 128])
        else:
            pieces.append(jnp.zeros((ROWS, 128), F32))
        fine[128 * b : 128 * b + 128, :] = jnp.concatenate(pieces, axis=0).T

    group = (lax.broadcasted_iota(I32, (128, 128), 1) // ROWS).astype(F32)

    def tabulate(f_ref, w_ref, base):
        def body(b, carry):
            packed = jnp.concatenate([w_ref[b], (f_ref[b] // SEG).astype(F32)], axis=0).T
            for k in range(K):
                weights = jnp.where(packed[:, K + k : K + k + 1] == group, packed[:, k : k + 1], 0.0)
                row = pl.multiple_of((base + b) * (K * 128) + k * 128, 128)
                table[pl.ds(row, 128), :] = weights
            return carry

        return body

    def gather(idx_ref, base):
        def body(t, carry):
            b = t // (128 // UNROLL)
            first = lax.rem(t, 128 // UNROLL) * UNROLL
            for u in range(UNROLL):
                terms = []
                for k in range(K):
                    at = idx_ref[b, k, first + u]
                    row = (base + b) * (K * 128) + k * 128 + first + u
                    terms.append(fine[pl.ds(at, 1), :] * table[pl.ds(row, 1), :])
                while len(terms) > 1:
                    terms = [terms[i] + terms[i + 1] for i in range(0, len(terms), 2)]
                acc[pl.ds((base + b) * 128 + first + u, 1), :] = terms[0]
            return carry

        return body

    def folded(b):
        flat = acc[128 * b : 128 * b + 128, :].T
        total = flat[0:ROWS]
        for g in range(1, 128 // ROWS):
            total = total + flat[ROWS * g : ROWS * g + ROWS]
        return total

    per = 128 // UNROLL
    lax.fori_loop(0, OWN, tabulate(f_own, w_own, 0), 0)
    own_index.wait()
    ahead = 24
    lax.fori_loop(0, ahead, gather(idx_own, 0), 0)

    for copy in lists:
        copy.wait()
    for b in range(FOREIGN):
        r_for[b] = f_for[b] & (SEG - 1)
    for_index = pltpu.make_async_copy(r_for, idx_for, local_sem.at[12])
    for_index.start()
    lax.fori_loop(0, FOREIGN, tabulate(f_for, w_for, OWN), 0)
    acc[(OWN + half - 1) * 128 : (OWN + half + 1) * 128, :] = jnp.zeros((256, 128), F32)
    for_index.wait()
    lax.fori_loop(0, 2 * per + 1, gather(idx_for, OWN), 0)
    for b in range(half):
        sum_out[0, :, 128 * b : 128 * b + 128] = folded(OWN + b)
    sums = [send(sum_out.at[0], sum_in.at[0], 8, to_right)]
    lax.fori_loop((half + 1) * per - 1, FOREIGN * per, gather(idx_for, OWN), 0)
    for b in range(half):
        sum_out[1, :, 128 * b : 128 * b + 128] = folded(OWN + half + b)
    sums.append(send(sum_out.at[1], sum_in.at[1], 9, to_left))

    lax.fori_loop(ahead, OWN * per, gather(idx_own, 0), 0)
    for b in range(OWN):
        restricted[:, 128 * b : 128 * b + 128] = folded(b)

    for i in range(6, 9):
        loads[i].wait()
    spots = (nbr[...] - tile * COLS + HALO) & (tiles * COLS - 1)
    for side in range(2):
        for b in range(COLS // WIDE):
            where = spots[2 + side : 3 + side, WIDE * b : WIDE * b + WIDE] - (WIDE * b + HALO * side)
            hit = lax.broadcasted_iota(I32, (REACH, WIDE), 0) == where
            onehot[side, b] = jnp.where(hit, 1.0, 0.0).astype(BF16)

    for copy in halos:
        copy.wait()
    parts[...] = halves(inc[...])
    mid = inc[:, HALO : HALO + COLS]
    row = lax.broadcasted_iota(I32, (ROWS, COLS), 0)
    couplings = vc[...]
    below_row = jnp.where(slab > 0, below[0:1, :], 0.0)
    below_coupling = jnp.where(slab > 0, below[1:2, :], 0.0)
    above_row = jnp.where(slab < slabs - 1, above[...], 0.0)
    couplings_down = jnp.where(row == 0, below_coupling, pltpu.roll(couplings, 1, 0))

    def vertical(value, under, over):
        up = jnp.where(row == ROWS - 1, over, pltpu.roll(value, ROWS - 1, 0))
        down = jnp.where(row == 0, under, pltpu.roll(value, 1, 0))
        return couplings * up + couplings_down * down

    image = cen[...] * mid + vertical(mid, below_row, above_row)
    around = inc[:, HALO - 128 : HALO + COLS + 128]
    image = image + cpl[0:1, :] * pltpu.roll(around, 1, 1)[:, 128 : 128 + COLS]
    image = image + cpl[1:2, :] * pltpu.roll(around, COLS + 255, 1)[:, 128 : 128 + COLS]
    blocks = []
    for b in range(COLS // WIDE):
        total = None
        for side in range(2):
            start = WIDE * b + HALO * side
            got = jnp.dot(parts[:, start : start + REACH], onehot[side, b], preferred_element_type=F32)
            term = cpl[2 + side : 3 + side, WIDE * b : WIDE * b + WIDE] * (got[0:ROWS] + got[ROWS : 2 * ROWS])
            total = term if total is None else total + term
        blocks.append(total)
    image = image + jnp.concatenate(blocks, axis=1)

    for i in range(9, 11):
        loads[i].wait()
    prods[...] = jnp.zeros((128, 128), F32)
    slot = {}
    for i in range(M):
        y_i = grads[i].astype(F32)
        s_i = steps[i].astype(F32)
        for j in range(i, M):
            y_j = grads[j].astype(F32)
            for name, value in (("sy", s_i), ("yy", y_i)):
                slot[name, i, j] = len(slot)
                at = slot[name, i, j]
                prods[at : at + 1, :] = lane_sums(value * y_j)

    for copy in sums:
        copy.wait()
    restricted[:, 0:EDGE] = restricted[:, 0:EDGE] + sum_in[0]
    restricted[:, COLS - EDGE : COLS] = restricted[:, COLS - EDGE : COLS] + sum_in[1]
    misfit = image - restricted[...]
    mis_out[0] = misfit[ROWS - 1 : ROWS, :]
    mis_out[1] = misfit[0:1, :]
    edges = [
        send(mis_out.at[0], mis_in.at[0], 10, to_upper),
        send(mis_out.at[1], mis_in.at[1], 11, to_lower),
    ]

    spread[...] = jnp.zeros((ROWS, EXT), F32)
    blank = jnp.zeros((ROWS, 128), F32)
    back = jnp.concatenate([blank, cpl[0:1, :] * misfit, blank], axis=1)
    forth = jnp.concatenate([blank, cpl[1:2, :] * misfit, blank], axis=1)
    spread[:, HALO - 128 : HALO + COLS + 128] = pltpu.roll(back, COLS + 255, 1) + pltpu.roll(forth, 1, 1)
    for b in range(COLS // WIDE):
        for side in range(2):
            start = WIDE * b + HALO * side
            carried = halves(cpl[2 + side : 3 + side, WIDE * b : WIDE * b + WIDE] * misfit[:, WIDE * b : WIDE * b + WIDE])
            out = lax.dot_general(
                carried, onehot[side, b], (((1,), (1,)), ((), ())), preferred_element_type=F32
            )
            spread[:, start : start + REACH] = spread[:, start : start + REACH] + (out[0:ROWS] + out[ROWS : 2 * ROWS])
    rims = [
        send(spread.at[:, 0:HALO], rim_in.at[1], 12, to_left),
        send(spread.at[:, HALO + COLS : EXT], rim_in.at[0], 13, to_right),
    ]
    for copy in edges:
        copy.wait()
    under = jnp.where(slab > 0, mis_in[0], 0.0)
    over = jnp.where(slab < slabs - 1, mis_in[1], 0.0)
    gradient = mid + (cen[...] * misfit + vertical(misfit, under, over) + spread[:, HALO : HALO + COLS])
    for copy in rims:
        copy.wait()
    gradient = gradient + jnp.concatenate([rim_in[0], rim_in[1]], axis=1)
    gradient_ref[...] = gradient

    for i in range(M):
        for name, value in (("sg", steps[i]), ("yg", grads[i])):
            slot[name, i] = len(slot)
            at = slot[name, i]
            prods[at : at + 1, :] = lane_sums(value.astype(F32) * gradient)

    def reduced(value, buf, me, peers, sends, recvs):
        count = len(peers) + 1
        buf[me] = value
        copies = []
        for d, peer in enumerate(peers):
            copy = pltpu.make_async_remote_copy(
                src_ref=buf.at[me],
                dst_ref=buf.at[me],
                send_sem=sends.at[d],
                recv_sem=recvs.at[d],
                device_id=peer,
                device_id_type=pl.DeviceIdType.MESH,
            )
            copy.start()
            copies.append(copy)
        for copy in copies:
            copy.wait()
        total = buf[0]
        for i in range(1, count):
            total = total + buf[i]
        return total

    total = jnp.sum(prods[...].T, axis=0, keepdims=True)
    total = reduced(total, red_lev, slab, lev_peers, lev_send, lev_recv)
    total = reduced(total, red_y, row_y, y_peers, y_send, y_recv)
    total = reduced(total, red_z, row_z, z_peers, z_send, z_recv)

    spreaded = jnp.broadcast_to(total, (128, 128)).T
    of = {name: spreaded[at : at + 1, :] for name, at in slot.items()}
    rho = [1.0 / of["sy", i, i] for i in range(M)]
    alpha = [None] * M
    for i in range(M - 1, -1, -1):
        value = of["sg", i]
        for j in range(i + 1, M):
            value = value - alpha[j] * of["sy", i, j]
        alpha[i] = rho[i] * value
    gamma = of["sy", M - 1, M - 1] / of["yy", M - 1, M - 1]
    keep = []
    for i in range(M):
        value = of["yg", i]
        for j in range(M):
            value = value - alpha[j] * of["yy", min(i, j), max(i, j)]
        value = gamma * value
        for j in range(i):
            value = value + keep[j] * of["sy", j, i]
        keep.append(alpha[i] - rho[i] * value)

    def wide(value):
        return jnp.concatenate([value] * (COLS // 128), axis=1)

    result = wide(-gamma) * gradient_ref[...]
    for i in range(M):
        result = result + wide(gamma * alpha[i]) * grads[i].astype(F32)
        result = result - wide(keep[i]) * steps[i].astype(F32)
    direction_ref[...] = result


def per_device(tiles, slabs, *args):
    (dep, off, wgt, cnt, inc, cen, vc, nbr, cpl, steps, grads) = args
    cnt = cnt.reshape(1, COLS)
    vmem = pltpu.VMEM
    sems = pltpu.SemaphoreType.DMA
    nz = tiles // NY
    shape = jax.ShapeDtypeStruct((ROWS, COLS), F32)
    return pl.pallas_call(
        functools.partial(kernel, tiles, slabs),
        out_shape=(shape, shape),
        in_specs=[pl.BlockSpec(memory_space=pl.ANY)] * 11,
        out_specs=[pl.BlockSpec(memory_space=vmem)] * 2,
        scratch_shapes=[
            vmem((ROWS, FINE), F32),
            vmem((K, COLS), I32),
            vmem((K, COLS), F32),
            vmem((1, COLS), I32),
            vmem((ROWS, COLS), F32),
            vmem((ROWS, COLS), F32),
            vmem((4, COLS), I32),
            vmem((4, COLS), F32),
            vmem((M, ROWS, COLS), BF16),
            vmem((M, ROWS, COLS), BF16),
            vmem((SEG, 128), F32),
            vmem(((OWN + FOREIGN) * K * 128, 128), F32),
            vmem(((OWN + FOREIGN) * 128, 128), F32),
            vmem((OWN, K, 128), I32),
            vmem((OWN, K, 128), F32),
            vmem((OWN, K, 128), I32),
            vmem((FOREIGN, K, 128), I32),
            vmem((FOREIGN, K, 128), F32),
            vmem((FOREIGN, K, 128), I32),
            vmem((FOREIGN, K, 128), F32),
            vmem((FOREIGN, K, 128), I32),
            pltpu.SMEM((OWN, K, 128), I32),
            pltpu.SMEM((FOREIGN, K, 128), I32),
            vmem((ROWS, EXT), F32),
            vmem((2 * ROWS, EXT), BF16),
            vmem((2, COLS // WIDE, REACH, WIDE), BF16),
            vmem((2, COLS), F32),
            vmem((2, COLS), F32),
            vmem((1, COLS), F32),
            vmem((1, COLS), F32),
            vmem((2, ROWS, EDGE), F32),
            vmem((2, ROWS, EDGE), F32),
            vmem((ROWS, COLS), F32),
            vmem((2, 1, COLS), F32),
            vmem((2, 1, COLS), F32),
            vmem((ROWS, EXT), F32),
            vmem((2, ROWS, HALO), F32),
            vmem((128, 128), F32),
            vmem((slabs, 1, 128), F32),
            vmem((NY, 1, 128), F32),
            vmem((nz, 1, 128), F32),
            sems((13,)),
            sems((14,)),
            sems((14,)),
            sems((slabs,)),
            sems((slabs,)),
            sems((NY,)),
            sems((NY,)),
            sems((nz,)),
            sems((nz,)),
        ],
        compiler_params=pltpu.CompilerParams(
            collective_id=0, has_side_effects=True, vmem_limit_bytes=48 * 1024 * 1024
        ),
        cost_estimate=pl.CostEstimate(flops=1 << 28, bytes_accessed=1 << 22, transcendentals=0),
    )(dep, off, wgt, cnt, inc, cen, vc, nbr, cpl, steps, grads)


def solution(mesh):
    tiles, slabs = mesh.shape["cols"], mesh.shape["lev"]
    return jax.shard_map(
        functools.partial(per_device, tiles, slabs),
        mesh=mesh,
        in_specs=(
            P("lev", "cols"),
            P(None, "cols"),
            P(None, "cols"),
            P("cols"),
            P("lev", "cols"),
            P("lev", "cols"),
            P("lev", "cols"),
            P(None, "cols"),
            P(None, "cols"),
            P(None, "lev", "cols"),
            P(None, "lev", "cols"),
        ),
        out_specs=(P("lev", "cols"), P("lev", "cols")),
        check_vma=False,
    )
```

time: 879 us -> 70.8 us (0.08)
  blocking collectives: 597 us -> 0 us
  local copies, waits for them, and re-layouts: 154 us -> 10.8 us
  other arithmetic: 87.4 us -> 0 us
  Pallas kernels: 0 us -> 58.8 us
  starting transfers between devices: 22.3 us -> 0 us
  between operations: 12.8 us -> 0.66 us
    psum x8 -> x0, blocking collectives: 597 us -> none  [the longest x7 517 us: inner_product(): return lax.psum(jnp.sum(first * second), ('cols', 'lev'))]
    gather x12 -> x0, local copies, waits for them, and re-layouts: 113 us -> none  [the longest x8 95.9 us: per_device(): jnp.take(extended, local_index[entry], axis=1)]
    pallas_call x0 -> x1, Pallas kernels: none -> 58.8 us  [per_device(): pl.pallas_call(functools.partial(kernel, tiles, slabs), out_shape=(shape,...]
    scatter-add x6 -> x0, other arithmetic: 36.6 us -> none  [the longest x4 32.5 us: per_device(): spread_back.at[:, neighbor_local[side]].add(couple[side][None, :] * misfit)]
    ppermute x10 -> x0, starting transfers between devices: 22.3 us -> none  [the longest x4 8.82 us: padded_2(): lax.ppermute(tail, axis, [(i, (i + 1) % count) for i in range(ends)])]
    slice x24 -> x0, local copies, waits for them, and re-layouts: 17 us -> none  [the longest x4 4.97 us: padded_2(): lax.slice_in_dim(cells, cells.shape[dim] - width, cells.shape[dim], axis=...]
    reduce_sum x11 -> x0, other arithmetic: 14.4 us -> none  [the longest x7 11.3 us: inner_product(): return lax.psum(jnp.sum(first * second), ('cols', 'lev'))]
    concatenate x2 -> x0, local copies, waits for them, and re-layouts: 13.1 us -> none  [padded_2(): jnp.concatenate([lax.ppermute(tail, axis, [(i, (i + 1) % count) for i in...]
  transfers between devices with their start and end apart: 10 -> 0, of which waited for: 0 -> 0; matrix products, arithmetic and copies ran while one was open for 11% -> 0% of each run, Pallas kernels for 0% -> 0%
where the time goes in v1:
time: 70.8 us; the launch traced here: 70.2 us
  Pallas kernels  58.8 us (83%)
  local copies, waits for them, and re-layouts  10.8 us (15%)
    pallas_call x1, Pallas kernels, per_device(): pl.pallas_call(functools.partial(kernel, tiles, slabs), out_shape=(shape,...  58.8 us
    unnamed x24, local copies, waits for them, and re-layouts  10.8 us

profile of v1, /device:TPU:8, one launch (start us, length us, event | category | flops | bytes accessed | tf_op | source)
XLA Modules:
  0.0 70.2 jit_solution(16887711009276926625)
XLA Ops:
  0.6 0.0 copy-start
  0.6 1.6 %copy-done = f32[16,31744]{1,0:T(8,128)S(1)} copy-done((f32[16,31744]{1,0:T(8,128)S(1)}, f32[16,31744]{1,0:T(8,128)}, u32[]{:S(2)}) %copy-start) | copy-done | bytes 2031640
  2.2 0.0 copy-start.1
  2.2 0.9 %copy-done.1 = bf16[4,16,1024]{2,1,0:T(8,128)(2,1)S(1)} copy-done((bf16[4,16,1024]{2,1,0:T(8,128)(2,1)S(1)}, bf16[4,16,1024]{2,1,0:T(8,128)(2,1)}, u32[]{:S(2)}) %copy-start.1) | copy-done | bytes 131096
  3.1 0.0 copy-start.2
  3.1 0.9 %copy-done.2 = bf16[4,16,1024]{2,1,0:T(8,128)(2,1)S(1)} copy-done((bf16[4,16,1024]{2,1,0:T(8,128)(2,1)S(1)}, bf16[4,16,1024]{2,1,0:T(8,128)(2,1)}, u32[]{:S(2)}) %copy-start.2) | copy-done | bytes 131096
  4.0 0.0 copy-start.3
  4.0 0.8 %copy-done.3 = f32[16,1024]{1,0:T(8,128)S(1)} copy-done((f32[16,1024]{1,0:T(8,128)S(1)}, f32[16,1024]{1,0:T(8,128)}, u32[]{:S(2)}) %copy-start.3) | copy-done | bytes 65560
  4.9 0.0 copy-start.4
  4.9 0.8 %copy-done.4 = f32[16,1024]{1,0:T(8,128)S(1)} copy-done((f32[16,1024]{1,0:T(8,128)S(1)}, f32[16,1024]{1,0:T(8,128)}, u32[]{:S(2)}) %copy-start.4) | copy-done | bytes 65560
  5.7 0.0 copy-start.5
  5.7 0.8 %copy-done.5 = f32[16,1024]{1,0:T(8,128)S(1)} copy-done((f32[16,1024]{1,0:T(8,128)S(1)}, f32[16,1024]{1,0:T(8,128)}, u32[]{:S(2)}) %copy-start.5) | copy-done | bytes 65560
  6.5 0.0 copy-start.6
  6.5 0.8 %copy-done.6 = s32[8,1024]{1,0:T(8,128)S(1)} copy-done((s32[8,1024]{1,0:T(8,128)S(1)}, s32[8,1024]{1,0:T(8,128)}, u32[]{:S(2)}) %copy-start.6) | copy-done | bytes 32792
  7.3 0.0 copy-start.7
  7.3 0.8 %copy-done.7 = f32[8,1024]{1,0:T(8,128)S(1)} copy-done((f32[8,1024]{1,0:T(8,128)S(1)}, f32[8,1024]{1,0:T(8,128)}, u32[]{:S(2)}) %copy-start.7) | copy-done | bytes 32792
  8.0 0.0 copy-start.8
  8.1 0.7 %copy-done.8 = s32[4,1024]{1,0:T(4,128)S(1)} copy-done((s32[4,1024]{1,0:T(4,128)S(1)}, s32[4,1024]{1,0:T(4,128)}, u32[]{:S(2)}) %copy-start.8) | copy-done | bytes 16408
  8.8 0.0 copy-start.9
  8.8 0.7 %copy-done.9 = f32[4,1024]{1,0:T(4,128)S(1)} copy-done((f32[4,1024]{1,0:T(4,128)S(1)}, f32[4,1024]{1,0:T(4,128)}, u32[]{:S(2)}) %copy-start.9) | copy-done | bytes 16408
  9.5 0.0 copy-start.10
  9.5 0.7 copy-done.10
  10.2 58.8 %shard_map.122 = (f32[16,1024]{1,0:T(8,128)S(1)}, f32[16,1024]{1,0:T(8,128)S(1)}) custom-call(f32[16,31744]{1,0:T(8,128)S(1)} %copy-done, s32[8,1024]{1,0:T(8,128)S(1)} %copy-done.6, f32[8,1024]{1,0:T(8,128)S(1)} %copy-done.7, s32[1,1024]{1,0:T(1,128)S(1)} %bitcast.1, f32[16,1024]{1,0:T(8,128)S(1)} %copy-done.3, f32[16,1024]{1,0:T(8,128)S(1)} %copy-done.4, ...), custom_call_target="tpu_custom_call" | custom-call | flops 268435456 | bytes 4194304 | tf_op jit(solution)/shard_map/pallas_call | solution.py:450
  69.0 0.6 copy.15
  69.6 0.6 copy.16
Async XLA Ops:
  0.6 1.6 %copy-start = (f32[16,31744]{1,0:T(8,128)S(1)}, f32[16,31744]{1,0:T(8,128)}, u32[]{:S(2)}) copy-start(f32[16,31744]{1,0:T(8,128)} %dep_hbm.1) | copy-start | bytes 6094852
  2.2 0.9 %copy-start.1 = (bf16[4,16,1024]{2,1,0:T(8,128)(2,1)S(1)}, bf16[4,16,1024]{2,1,0:T(8,128)(2,1)}, u32[]{:S(2)}) copy-start(bf16[4,16,1024]{2,1,0:T(8,128)(2,1)} %step_hbm.1) | copy-start | bytes 393220
  3.1 0.9 %copy-start.2 = (bf16[4,16,1024]{2,1,0:T(8,128)(2,1)S(1)}, bf16[4,16,1024]{2,1,0:T(8,128)(2,1)}, u32[]{:S(2)}) copy-start(bf16[4,16,1024]{2,1,0:T(8,128)(2,1)} %grad_hbm.1) | copy-start | bytes 393220
  4.0 0.8 %copy-start.3 = (f32[16,1024]{1,0:T(8,128)S(1)}, f32[16,1024]{1,0:T(8,128)}, u32[]{:S(2)}) copy-start(f32[16,1024]{1,0:T(8,128)} %inc_hbm.1) | copy-start | bytes 196612
  4.9 0.8 %copy-start.4 = (f32[16,1024]{1,0:T(8,128)S(1)}, f32[16,1024]{1,0:T(8,128)}, u32[]{:S(2)}) copy-start(f32[16,1024]{1,0:T(8,128)} %cen_hbm.1) | copy-start | bytes 196612
  5.7 0.8 %copy-start.5 = (f32[16,1024]{1,0:T(8,128)S(1)}, f32[16,1024]{1,0:T(8,128)}, u32[]{:S(2)}) copy-start(f32[16,1024]{1,0:T(8,128)} %vc_hbm.1) | copy-start | bytes 196612
  6.5 0.8 %copy-start.6 = (s32[8,1024]{1,0:T(8,128)S(1)}, s32[8,1024]{1,0:T(8,128)}, u32[]{:S(2)}) copy-start(s32[8,1024]{1,0:T(8,128)} %off_hbm.1) | copy-start | bytes 98308
  7.3 0.8 %copy-start.7 = (f32[8,1024]{1,0:T(8,128)S(1)}, f32[8,1024]{1,0:T(8,128)}, u32[]{:S(2)}) copy-start(f32[8,1024]{1,0:T(8,128)} %wgt_hbm.1) | copy-start | bytes 98308
  8.0 0.7 %copy-start.8 = (s32[4,1024]{1,0:T(4,128)S(1)}, s32[4,1024]{1,0:T(4,128)}, u32[]{:S(2)}) copy-start(s32[4,1024]{1,0:T(4,128)} %nbr_hbm.1) | copy-start | bytes 49156
  8.8 0.7 %copy-start.9 = (f32[4,1024]{1,0:T(4,128)S(1)}, f32[4,1024]{1,0:T(4,128)}, u32[]{:S(2)}) copy-start(f32[4,1024]{1,0:T(4,128)} %cpl_hbm.1) | copy-start | bytes 49156
  9.5 0.7 copy-start.10

commit v2 on v1

--- a/solution.py
+++ b/solution.py
@@ -18,8 +18,8 @@
 EXT = COLS + 2 * HALO
 EDGE = 384
 OWN = COLS // 128
-FOREIGN = 2 * EDGE // 128
-UNROLL = 16
+FOREIGN = 5
+EARLY = 3
 WIDE = 256
 REACH = WIDE + HALO
 NY = 4
@@ -69,18 +69,17 @@
     steps,
     grads,
     fine,
-    table,
-    acc,
-    f_own,
-    w_own,
-    r_own,
+    rows_a,
+    rows_b,
+    result,
+    f_all,
+    w_all,
+    r_all,
     f_out,
     w_out,
     f_for,
     w_for,
-    r_for,
-    idx_own,
-    idx_for,
+    index,
     inc,
     parts,
     onehot,
@@ -90,7 +89,6 @@
     above,
     sum_out,
     sum_in,
-    restricted,
     mis_out,
     mis_in,
     spread,
@@ -126,8 +124,8 @@
     y_peers = [spot(row_z * NY + lax.rem(row_y + d, NY), slab) for d in range(1, NY)]
     z_peers = [spot(lax.rem(row_z + d, nz) * NY + row_y, slab) for d in range(1, nz)]
 
-    def send(src, dst, i, target):
-        copy = pltpu.make_async_remote_copy(
+    def remote(src, dst, i, target):
+        return pltpu.make_async_remote_copy(
             src_ref=src,
             dst_ref=dst,
             send_sem=send_sem.at[i],
@@ -135,6 +133,9 @@
             device_id=target,
             device_id_type=pl.DeviceIdType.MESH,
         )
+
+    def send(src, dst, i, target):
+        copy = remote(src, dst, i, target)
         copy.start()
         return copy
 
@@ -166,6 +167,7 @@
     for i in range(5):
         loads[i].wait()
 
+    half = EDGE // 128
     lane = lax.broadcasted_iota(I32, (8, 128), 1)
     entry = lax.broadcasted_iota(I32, (8, 128), 0)
     for b in range(OWN):
@@ -174,17 +176,17 @@
         w = jnp.where(entry < cnt[:, cut], wgt[:, cut], 0.0)
         here = (f >= 0) & (f < FINE)
         fo = jnp.where(here, f, 0)
-        f_own[b] = fo
-        r_own[b] = fo & (SEG - 1)
-        w_own[b] = jnp.where(here, w, 0.0)
-        if b < FOREIGN // 2:
+        f_all[b] = fo
+        r_all[b * K : (b + 1) * K, :] = fo & (SEG - 1)
+        w_all[b] = jnp.where(here, w, 0.0)
+        if b < half:
             f_out[b] = jnp.where(f < 0, f + FINE, 0)
             w_out[b] = jnp.where(f < 0, w, 0.0)
-        if b >= OWN - FOREIGN // 2:
-            at = b - OWN + FOREIGN
+        if b >= OWN - half:
+            at = b - OWN + 2 * half
             f_out[at] = jnp.where(f >= FINE, f - FINE, 0)
             w_out[at] = jnp.where(f >= FINE, w, 0.0)
-    own_index = pltpu.make_async_copy(r_own, idx_own, local_sem.at[11])
+    own_index = pltpu.make_async_copy(r_all.at[0 : OWN * K], index.at[0 : OWN * K], local_sem.at[11])
     own_index.start()
     up_out[0:1, :] = inc[ROWS - 1 : ROWS, HALO : HALO + COLS]
     up_out[1:2, :] = vc[ROWS - 1 : ROWS, :]
@@ -192,14 +194,13 @@
 
     pl.semaphore_wait(barrier, len(greeted))
 
-    half = FOREIGN // 2
     to_left, to_right = spot(left, slab), spot(right, slab)
     to_lower, to_upper = spot(tile, lower), spot(tile, upper)
     lists = [
         send(f_out.at[0:half], f_for.at[0:half], 0, to_left),
         send(w_out.at[0:half], w_for.at[0:half], 1, to_left),
-        send(f_out.at[half:FOREIGN], f_for.at[half:FOREIGN], 2, to_right),
-        send(w_out.at[half:FOREIGN], w_for.at[half:FOREIGN], 3, to_right),
+        send(f_out.at[half : 2 * half], f_for.at[half : 2 * half], 2, to_right),
+        send(w_out.at[half : 2 * half], w_for.at[half : 2 * half], 3, to_right),
     ]
     halos = [
         send(inc.at[:, HALO : 2 * HALO], inc.at[:, HALO + COLS : EXT], 4, to_left),
@@ -219,70 +220,81 @@
             pieces.append(jnp.zeros((ROWS, 128), F32))
         fine[128 * b : 128 * b + 128, :] = jnp.concatenate(pieces, axis=0).T
 
-    group = (lax.broadcasted_iota(I32, (128, 128), 1) // ROWS).astype(F32)
-
-    def tabulate(f_ref, w_ref, base):
-        def body(b, carry):
-            packed = jnp.concatenate([w_ref[b], (f_ref[b] // SEG).astype(F32)], axis=0).T
+    def gather(b, rows, lanes):
+        for u in lanes:
             for k in range(K):
-                weights = jnp.where(packed[:, K + k : K + k + 1] == group, packed[:, k : k + 1], 0.0)
-                row = pl.multiple_of((base + b) * (K * 128) + k * 128, 128)
-                table[pl.ds(row, 128), :] = weights
-            return carry
-
-        return body
-
-    def gather(idx_ref, base):
-        def body(t, carry):
-            b = t // (128 // UNROLL)
-            first = lax.rem(t, 128 // UNROLL) * UNROLL
-            for u in range(UNROLL):
-                terms = []
-                for k in range(K):
-                    at = idx_ref[b, k, first + u]
-                    row = (base + b) * (K * 128) + k * 128 + first + u
-                    terms.append(fine[pl.ds(at, 1), :] * table[pl.ds(row, 1), :])
-                while len(terms) > 1:
-                    terms = [terms[i] + terms[i + 1] for i in range(0, len(terms), 2)]
-                acc[pl.ds((base + b) * 128 + first + u, 1), :] = terms[0]
-            return carry
-
-        return body
-
-    def folded(b):
-        flat = acc[128 * b : 128 * b + 128, :].T
-        total = flat[0:ROWS]
-        for g in range(1, 128 // ROWS):
-            total = total + flat[ROWS * g : ROWS * g + ROWS]
+                rows[k * 128 + u : k * 128 + u + 1, :] = fine[pl.ds(index[b * K + k, u], 1), :]
+
+    def weighed(b, rows):
+        segment = f_all[b] // SEG
+        weights = w_all[b]
+        chosen = [jnp.where(segment == g, weights, 0.0) for g in range(8)]
+        total = jnp.zeros((ROWS, 128), F32)
+        for k in range(K):
+            flat = rows[128 * k : 128 * k + 128, :].T
+            for g in range(8):
+                total = total + chosen[g][k : k + 1, :] * flat[ROWS * g : ROWS * g + ROWS]
         return total
 
-    per = 128 // UNROLL
-    lax.fori_loop(0, OWN, tabulate(f_own, w_own, 0), 0)
+    def block_of(i):
+        return jnp.where(i < EARLY, 2 * i, jnp.where(i < EARLY + 2, OWN + 2 * (i - EARLY), 2 * (i - 2)))
+
+    for_index = pltpu.make_async_copy(
+        r_all.at[OWN * K : (OWN + FOREIGN) * K], index.at[OWN * K : (OWN + FOREIGN) * K], local_sem.at[12]
+    )
+    edge = OWN + FOREIGN - 1
+
+    def pair(i, carry):
+        @pl.when(i == EARLY - 1)
+        def _():
+            for copy in lists:
+                copy.wait()
+            for at, b in enumerate((0, 1, 4, 5)):
+                f_all[OWN + at] = f_for[b]
+                w_all[OWN + at] = w_for[b]
+                r_all[(OWN + at) * K : (OWN + at + 1) * K, :] = f_for[b] & (SEG - 1)
+            f_all[edge] = jnp.where(lane < 64, f_for[2], f_for[3])
+            w_all[edge] = jnp.where(lane < 64, w_for[2], w_for[3])
+            r_all[edge * K : (edge + 1) * K, :] = f_all[edge] & (SEG - 1)
+            for_index.start()
+
+        @pl.when(i == EARLY)
+        def _():
+            for_index.wait()
+
+        @pl.when(i == EARLY + 2)
+        def _():
+            gather(edge, rows_a, [*range(16), *range(112, 128)])
+            far = weighed(edge - 1, rows_b)
+            rest = weighed(edge, rows_a)
+            at = lax.broadcasted_iota(I32, (ROWS, 128), 1)
+            sum_out[0, :, 0:128] = result[OWN]
+            sum_out[0, :, 128:256] = result[OWN + 1]
+            sum_out[0, :, 256:384] = jnp.where(at < 64, rest, 0.0)
+            sum_out[1, :, 0:128] = jnp.where(at < 64, 0.0, rest)
+            sum_out[1, :, 128:256] = result[OWN + 2]
+            sum_out[1, :, 256:384] = far
+            for copy in sums:
+                copy.start()
+
+        b = block_of(i)
+        before = jnp.where(i == 0, edge + 1, block_of(i - 1) + 1)
+        gather(b, rows_a, range(128))
+        result[before] = weighed(before, rows_b)
+        gather(b + 1, rows_b, range(128))
+        result[b] = weighed(b, rows_a)
+        return carry
+
+    sums = [
+        remote(sum_out.at[0], sum_in.at[0], 8, to_right),
+        remote(sum_out.at[1], sum_in.at[1], 9, to_left),
+    ]
     own_index.wait()
-    ahead = 24
-    lax.fori_loop(0, ahead, gather(idx_own, 0), 0)
-
-    for copy in lists:
-        copy.wait()
-    for b in range(FOREIGN):
-        r_for[b] = f_for[b] & (SEG - 1)
-    for_index = pltpu.make_async_copy(r_for, idx_for, local_sem.at[12])
-    for_index.start()
-    lax.fori_loop(0, FOREIGN, tabulate(f_for, w_for, OWN), 0)
-    acc[(OWN + half - 1) * 128 : (OWN + half + 1) * 128, :] = jnp.zeros((256, 128), F32)
-    for_index.wait()
-    lax.fori_loop(0, 2 * per + 1, gather(idx_for, OWN), 0)
-    for b in range(half):
-        sum_out[0, :, 128 * b : 128 * b + 128] = folded(OWN + b)
-    sums = [send(sum_out.at[0], sum_in.at[0], 8, to_right)]
-    lax.fori_loop((half + 1) * per - 1, FOREIGN * per, gather(idx_for, OWN), 0)
-    for b in range(half):
-        sum_out[1, :, 128 * b : 128 * b + 128] = folded(OWN + half + b)
-    sums.append(send(sum_out.at[1], sum_in.at[1], 9, to_left))
-
-    lax.fori_loop(ahead, OWN * per, gather(idx_own, 0), 0)
-    for b in range(OWN):
-        restricted[:, 128 * b : 128 * b + 128] = folded(b)
+    f_all[edge + 1] = jnp.zeros((K, 128), I32)
+    w_all[edge + 1] = jnp.zeros((K, 128), F32)
+    rows_b[...] = jnp.zeros((K * 128, 128), F32)
+    lax.fori_loop(0, (OWN + FOREIGN - 1) // 2, pair, 0)
+    result[OWN - 1] = weighed(OWN - 1, rows_b)
 
     for i in range(6, 9):
         loads[i].wait()
@@ -340,9 +352,10 @@
 
     for copy in sums:
         copy.wait()
-    restricted[:, 0:EDGE] = restricted[:, 0:EDGE] + sum_in[0]
-    restricted[:, COLS - EDGE : COLS] = restricted[:, COLS - EDGE : COLS] + sum_in[1]
-    misfit = image - restricted[...]
+    blank = jnp.zeros((ROWS, COLS - 2 * EDGE), F32)
+    restricted = jnp.concatenate([result[b] for b in range(OWN)], axis=1)
+    restricted = restricted + jnp.concatenate([sum_in[0], blank, sum_in[1]], axis=1)
+    misfit = image - restricted
     mis_out[0] = misfit[ROWS - 1 : ROWS, :]
     mis_out[1] = misfit[0:1, :]
     edges = [
@@ -450,7 +463,7 @@
     return pl.pallas_call(
         functools.partial(kernel, tiles, slabs),
         out_shape=(shape, shape),
-        in_specs=[pl.BlockSpec(memory_space=pl.ANY)] * 11,
+        in_specs=[pl.BlockSpec(memory_space=pltpu.HBM)] * 11,
         out_specs=[pl.BlockSpec(memory_space=vmem)] * 2,
         scratch_shapes=[
             vmem((ROWS, FINE), F32),
@@ -464,18 +477,17 @@
             vmem((M, ROWS, COLS), BF16),
             vmem((M, ROWS, COLS), BF16),
             vmem((SEG, 128), F32),
-            vmem(((OWN + FOREIGN) * K * 128, 128), F32),
-            vmem(((OWN + FOREIGN) * 128, 128), F32),
-            vmem((OWN, K, 128), I32),
-            vmem((OWN, K, 128), F32),
-            vmem((OWN, K, 128), I32),
-            vmem((FOREIGN, K, 128), I32),
-            vmem((FOREIGN, K, 128), F32),
-            vmem((FOREIGN, K, 128), I32),
-            vmem((FOREIGN, K, 128), F32),
-            vmem((FOREIGN, K, 128), I32),
-            pltpu.SMEM((OWN, K, 128), I32),
-            pltpu.SMEM((FOREIGN, K, 128), I32),
+            vmem((K * 128, 128), F32),
+            vmem((K * 128, 128), F32),
+            vmem((OWN + FOREIGN + 1, ROWS, 128), F32),
+            vmem((OWN + FOREIGN + 1, K, 128), I32),
+            vmem((OWN + FOREIGN + 1, K, 128), F32),
+            vmem(((OWN + FOREIGN) * K, 128), I32),
+            vmem((2 * EDGE // 128, K, 128), I32),
+            vmem((2 * EDGE // 128, K, 128), F32),
+            vmem((2 * EDGE // 128, K, 128), I32),
+            vmem((2 * EDGE // 128, K, 128), F32),
+            pltpu.SMEM(((OWN + FOREIGN) * K, 128), I32),
             vmem((ROWS, EXT), F32),
             vmem((2 * ROWS, EXT), BF16),
             vmem((2, COLS // WIDE, REACH, WIDE), BF16),
@@ -485,7 +497,6 @@
             vmem((1, COLS), F32),
             vmem((2, ROWS, EDGE), F32),
             vmem((2, ROWS, EDGE), F32),
-            vmem((ROWS, COLS), F32),
             vmem((2, 1, COLS), F32),
             vmem((2, 1, COLS), F32),
             vmem((ROWS, EXT), F32),
@@ -505,7 +516,7 @@
             sems((nz,)),
         ],
         compiler_params=pltpu.CompilerParams(
-            collective_id=0, has_side_effects=True, vmem_limit_bytes=48 * 1024 * 1024
+            collective_id=0, has_side_effects=True, vmem_limit_bytes=60 * 1024 * 1024
         ),
         cost_estimate=pl.CostEstimate(flops=1 << 28, bytes_accessed=1 << 22, transcendentals=0),
     )(dep, off, wgt, cnt, inc, cen, vc, nbr, cpl, steps, grads)

time: 70.8 us -> 45.9 us (0.65)
  Pallas kernels: 58.8 us -> 42.1 us
  local copies, waits for them, and re-layouts: 10.8 us -> 2.95 us
    pallas_call x1, Pallas kernels: 58.8 us -> 42.1 us  [per_device(): pl.pallas_call(functools.partial(kernel, tiles, slabs), out_shape=(shape,...]
    unnamed x24 -> x2, local copies, waits for them, and re-layouts: 10.8 us -> 2.95 us
where the time goes in v2:
time: 45.9 us; the launch traced here: 45.7 us
  Pallas kernels  42.1 us (92%)
  local copies, waits for them, and re-layouts  2.95 us (6%)
  between operations  0.64 us (1%)
    pallas_call x1, Pallas kernels, per_device(): pl.pallas_call(functools.partial(kernel, tiles, slabs), out_shape=(shape,...  42.1 us
    unnamed x2, local copies, waits for them, and re-layouts  2.95 us

profile of v2, /device:TPU:8, one launch (start us, length us, event | category | flops | bytes accessed | tf_op | source)
XLA Modules:
  0.0 45.7 jit_solution(17705783208511710081)
XLA Ops:
  0.6 42.1 %shard_map.122 = (f32[16,1024]{1,0:T(8,128)}, f32[16,1024]{1,0:T(8,128)}) custom-call(f32[16,31744]{1,0:T(8,128)} %dep_hbm.1, s32[8,1024]{1,0:T(8,128)} %off_hbm.1, f32[8,1024]{1,0:T(8,128)} %wgt_hbm.1, s32[1,1024]{1,0:T(1,128)} %bitcast.1, f32[16,1024]{1,0:T(8,128)} %inc_hbm.1, f32[16,1024]{1,0:T(8,128)} %cen_hbm.1, f32[16,1024]{1,0:T(8,128)} %vc_hbm.1, ...), custom_call_target="tpu_custom_call" | custom-call | flops 268435456 | bytes 4194304 | tf_op jit(solution)/shard_map/pallas_call | solution.py:463
  42.8 1.5 %copy.15 = f32[16,1024]{1,0:T(8,128)} copy(f32[16,1024]{1,0:T(8,128)} %get-tuple-element.4) | data formatting | bytes 131072
  44.3 1.5 %copy.16 = f32[16,1024]{1,0:T(8,128)} copy(f32[16,1024]{1,0:T(8,128)} %get-tuple-element.5) | data formatting | bytes 131072

commit v3 on v2

--- a/solution.py
+++ b/solution.py
@@ -34,12 +34,15 @@
     return jnp.concatenate([high, low], axis=0)
 
 
-def lane_sums(value):
-    total = value[0:8] + value[8:16]
-    parts = [total[:, 128 * i : 128 * i + 128] for i in range(COLS // 128)]
+def lane_blocks(value):
+    parts = [value[:, 128 * i : 128 * i + 128] for i in range(value.shape[1] // 128)]
     while len(parts) > 1:
         parts = [parts[i] + parts[i + 1] for i in range(0, len(parts), 2)]
-    return jnp.sum(parts[0], axis=0, keepdims=True)
+    return parts[0]
+
+
+def lane_sums(value):
+    return jnp.sum(lane_blocks(value[0:8] + value[8:16]), axis=0, keepdims=True)
 
 
 def kernel(
@@ -56,8 +59,8 @@
     cpl_hbm,
     step_hbm,
     grad_hbm,
-    gradient_ref,
-    direction_ref,
+    gradient_hbm,
+    direction_hbm,
     dep,
     off,
     wgt,
@@ -79,7 +82,7 @@
     w_out,
     f_for,
     w_for,
-    index,
+    slots,
     inc,
     parts,
     onehot,
@@ -93,17 +96,22 @@
     mis_in,
     spread,
     rim_in,
+    pairs,
+    pair_up,
+    pair_below,
+    pair_down,
+    pair_above,
+    gradient,
+    direction,
     prods,
-    red_lev,
-    red_y,
+    red_plane,
     red_z,
     local_sem,
+    slot_sem,
     send_sem,
     recv_sem,
-    lev_send,
-    lev_recv,
-    y_send,
-    y_recv,
+    plane_send,
+    plane_recv,
     z_send,
     z_recv,
 ):
@@ -120,9 +128,16 @@
     def spot(column, level):
         return {"cols": column, "lev": level}
 
-    lev_peers = [spot(tile, lax.rem(slab + d, slabs)) for d in range(1, slabs)]
-    y_peers = [spot(row_z * NY + lax.rem(row_y + d, NY), slab) for d in range(1, NY)]
-    z_peers = [spot(lax.rem(row_z + d, nz) * NY + row_y, slab) for d in range(1, nz)]
+    def around(count):
+        return sorted(range(1, count), key=lambda d: -min(d, count - d))
+
+    plane_peers = [
+        spot(row_z * NY + lax.rem(row_y + e, NY), lax.rem(slab + d, slabs))
+        for e in around(NY) + [0]
+        for d in around(slabs) + [0]
+        if d or e
+    ]
+    z_peers = [spot(lax.rem(row_z + d, nz) * NY + row_y, slab) for d in around(nz)]
 
     def remote(src, dst, i, target):
         return pltpu.make_async_remote_copy(
@@ -160,7 +175,7 @@
         loads.append(copy)
 
     barrier = pltpu.get_barrier_semaphore()
-    greeted = lev_peers + y_peers + z_peers + [spot(left, slab), spot(right, slab)]
+    greeted = plane_peers + z_peers + [spot(left, slab), spot(right, slab)]
     for peer in greeted:
         pl.semaphore_signal(barrier, inc=1, device_id=peer, device_id_type=pl.DeviceIdType.MESH)
 
@@ -177,7 +192,7 @@
         here = (f >= 0) & (f < FINE)
         fo = jnp.where(here, f, 0)
         f_all[b] = fo
-        r_all[b * K : (b + 1) * K, :] = fo & (SEG - 1)
+        r_all[b] = fo & (SEG - 1)
         w_all[b] = jnp.where(here, w, 0.0)
         if b < half:
             f_out[b] = jnp.where(f < 0, f + FINE, 0)
@@ -186,8 +201,12 @@
             at = b - OWN + 2 * half
             f_out[at] = jnp.where(f >= FINE, f - FINE, 0)
             w_out[at] = jnp.where(f >= FINE, w, 0.0)
-    own_index = pltpu.make_async_copy(r_all.at[0 : OWN * K], index.at[0 : OWN * K], local_sem.at[11])
-    own_index.start()
+
+    def fetch(b, at):
+        return pltpu.make_async_copy(r_all.at[b], slots.at[at], slot_sem.at[at])
+
+    fetch(0, 0).start()
+    fetch(1, 1).start()
     up_out[0:1, :] = inc[ROWS - 1 : ROWS, HALO : HALO + COLS]
     up_out[1:2, :] = vc[ROWS - 1 : ROWS, :]
     down_out[...] = inc[0:1, HALO : HALO + COLS]
@@ -220,10 +239,25 @@
             pieces.append(jnp.zeros((ROWS, 128), F32))
         fine[128 * b : 128 * b + 128, :] = jnp.concatenate(pieces, axis=0).T
 
-    def gather(b, rows, lanes):
+    loads[9].wait()
+    loads[10].wait()
+    for i in range(M):
+        for at, value in ((i, steps[i]), (M + i, grads[i])):
+            field = value.astype(F32)
+            pairs[at, :, HALO : HALO + COLS] = field
+            pair_up[at : at + 1, :] = field[ROWS - 1 : ROWS]
+            pair_down[at : at + 1, :] = field[0:1]
+    halos += [
+        send(pairs.at[:, :, HALO : 2 * HALO], pairs.at[:, :, HALO + COLS : EXT], 14, to_left),
+        send(pairs.at[:, :, COLS : COLS + HALO], pairs.at[:, :, 0:HALO], 15, to_right),
+        send(pair_up, pair_below, 16, to_upper),
+        send(pair_down, pair_above, 17, to_lower),
+    ]
+
+    def gather(at, rows, lanes):
         for u in lanes:
             for k in range(K):
-                rows[k * 128 + u : k * 128 + u + 1, :] = fine[pl.ds(index[b * K + k, u], 1), :]
+                rows[k * 128 + u : k * 128 + u + 1, :] = fine[pl.ds(slots[at, k, u], 1), :]
 
     def weighed(b, rows):
         segment = f_all[b] // SEG
@@ -239,10 +273,8 @@
     def block_of(i):
         return jnp.where(i < EARLY, 2 * i, jnp.where(i < EARLY + 2, OWN + 2 * (i - EARLY), 2 * (i - 2)))
 
-    for_index = pltpu.make_async_copy(
-        r_all.at[OWN * K : (OWN + FOREIGN) * K], index.at[OWN * K : (OWN + FOREIGN) * K], local_sem.at[12]
-    )
     edge = OWN + FOREIGN - 1
+    turns = (OWN + FOREIGN - 1) // 2
 
     def pair(i, carry):
         @pl.when(i == EARLY - 1)
@@ -252,19 +284,16 @@
             for at, b in enumerate((0, 1, 4, 5)):
                 f_all[OWN + at] = f_for[b]
                 w_all[OWN + at] = w_for[b]
-                r_all[(OWN + at) * K : (OWN + at + 1) * K, :] = f_for[b] & (SEG - 1)
+                r_all[OWN + at] = f_for[b] & (SEG - 1)
             f_all[edge] = jnp.where(lane < 64, f_for[2], f_for[3])
             w_all[edge] = jnp.where(lane < 64, w_for[2], w_for[3])
-            r_all[edge * K : (edge + 1) * K, :] = f_all[edge] & (SEG - 1)
-            for_index.start()
-
-        @pl.when(i == EARLY)
-        def _():
-            for_index.wait()
+            r_all[edge] = f_all[edge] & (SEG - 1)
+            fetch(edge, 2).start()
 
         @pl.when(i == EARLY + 2)
         def _():
-            gather(edge, rows_a, [*range(16), *range(112, 128)])
+            fetch(edge, 2).wait()
+            gather(2, rows_a, [*range(16), *range(112, 128)])
             far = weighed(edge - 1, rows_b)
             rest = weighed(edge, rows_a)
             at = lax.broadcasted_iota(I32, (ROWS, 128), 1)
@@ -279,9 +308,14 @@
 
         b = block_of(i)
         before = jnp.where(i == 0, edge + 1, block_of(i - 1) + 1)
-        gather(b, rows_a, range(128))
+        later = jnp.where(i < turns - 1, block_of(i + 1), 0)
+        fetch(b, 0).wait()
+        gather(0, rows_a, range(128))
+        fetch(later, 0).start()
         result[before] = weighed(before, rows_b)
-        gather(b + 1, rows_b, range(128))
+        fetch(b + 1, 1).wait()
+        gather(1, rows_b, range(128))
+        fetch(later + 1, 1).start()
         result[b] = weighed(b, rows_a)
         return carry
 
@@ -289,11 +323,12 @@
         remote(sum_out.at[0], sum_in.at[0], 8, to_right),
         remote(sum_out.at[1], sum_in.at[1], 9, to_left),
     ]
-    own_index.wait()
     f_all[edge + 1] = jnp.zeros((K, 128), I32)
     w_all[edge + 1] = jnp.zeros((K, 128), F32)
     rows_b[...] = jnp.zeros((K * 128, 128), F32)
-    lax.fori_loop(0, (OWN + FOREIGN - 1) // 2, pair, 0)
+    lax.fori_loop(0, turns, pair, 0)
+    fetch(0, 0).wait()
+    fetch(1, 1).wait()
     result[OWN - 1] = weighed(OWN - 1, rows_b)
 
     for i in range(6, 9):
@@ -322,9 +357,9 @@
         return couplings * up + couplings_down * down
 
     image = cen[...] * mid + vertical(mid, below_row, above_row)
-    around = inc[:, HALO - 128 : HALO + COLS + 128]
-    image = image + cpl[0:1, :] * pltpu.roll(around, 1, 1)[:, 128 : 128 + COLS]
-    image = image + cpl[1:2, :] * pltpu.roll(around, COLS + 255, 1)[:, 128 : 128 + COLS]
+    near = inc[:, HALO - 128 : HALO + COLS + 128]
+    image = image + cpl[0:1, :] * pltpu.roll(near, 1, 1)[:, 128 : 128 + COLS]
+    image = image + cpl[1:2, :] * pltpu.roll(near, COLS + 255, 1)[:, 128 : 128 + COLS]
     blocks = []
     for b in range(COLS // WIDE):
         total = None
@@ -336,19 +371,14 @@
         blocks.append(total)
     image = image + jnp.concatenate(blocks, axis=1)
 
-    for i in range(9, 11):
-        loads[i].wait()
+    middle = slice(HALO, HALO + COLS)
     prods[...] = jnp.zeros((128, 128), F32)
     slot = {}
     for i in range(M):
-        y_i = grads[i].astype(F32)
-        s_i = steps[i].astype(F32)
         for j in range(i, M):
-            y_j = grads[j].astype(F32)
-            for name, value in (("sy", s_i), ("yy", y_i)):
-                slot[name, i, j] = len(slot)
-                at = slot[name, i, j]
-                prods[at : at + 1, :] = lane_sums(value * y_j)
+            for name, at in (("sy", i), ("yy", M + i)):
+                here = slot[name, i, j] = len(slot)
+                prods[here : here + 1, :] = lane_sums(pairs[at, :, middle] * pairs[M + j, :, middle])
 
     for copy in sums:
         copy.wait()
@@ -377,26 +407,40 @@
             )
             spread[:, start : start + REACH] = spread[:, start : start + REACH] + (out[0:ROWS] + out[ROWS : 2 * ROWS])
     rims = [
-        send(spread.at[:, 0:HALO], rim_in.at[1], 12, to_left),
-        send(spread.at[:, HALO + COLS : EXT], rim_in.at[0], 13, to_right),
-    ]
-    for copy in edges:
-        copy.wait()
-    under = jnp.where(slab > 0, mis_in[0], 0.0)
-    over = jnp.where(slab < slabs - 1, mis_in[1], 0.0)
-    gradient = mid + (cen[...] * misfit + vertical(misfit, under, over) + spread[:, HALO : HALO + COLS])
-    for copy in rims:
-        copy.wait()
-    gradient = gradient + jnp.concatenate([rim_in[0], rim_in[1]], axis=1)
-    gradient_ref[...] = gradient
-
-    for i in range(M):
-        for name, value in (("sg", steps[i]), ("yg", grads[i])):
-            slot[name, i] = len(slot)
-            at = slot[name, i]
-            prods[at : at + 1, :] = lane_sums(value.astype(F32) * gradient)
-
-    def reduced(value, buf, me, peers, sends, recvs):
+        send(spread.at[:, 0:HALO], rim_in.at[:, COLS - HALO : COLS], 12, to_left),
+        send(spread.at[:, HALO + COLS : EXT], rim_in.at[:, 0:HALO], 13, to_right),
+    ]
+    part = mid + (cen[...] * misfit + vertical(misfit, 0.0, 0.0) + spread[:, middle])
+
+    late = 24
+    to_below = below_coupling * misfit[0:1, :]
+    to_above = jnp.where(slab < slabs - 1, couplings[ROWS - 1 : ROWS, :] * misfit[ROWS - 1 : ROWS, :], 0.0)
+    beyond = lane_blocks(pair_below[...] * to_below + pair_above[...] * to_above)
+    sides = []
+    for at in range(2 * M):
+        total = lane_blocks(pairs[at, :, 0:HALO] * spread[:, 0:HALO])
+        total = total + lane_blocks(pairs[at, :, HALO + COLS : EXT] * spread[:, HALO + COLS : EXT])
+        total = total + lane_blocks(pairs[at, :, middle] * part)
+        sides.append(jnp.sum(total, axis=0, keepdims=True))
+        slot["sg" if at < M else "yg", at % M] = late + at
+    prods[late : late + 2 * M, :] = jnp.concatenate(sides, axis=0) + beyond
+
+    def finish():
+        for copy in edges:
+            copy.wait()
+        under = jnp.where(slab > 0, mis_in[0], 0.0)
+        over = jnp.where(slab < slabs - 1, mis_in[1], 0.0)
+        for copy in rims:
+            copy.wait()
+        whole = part + jnp.where(row == 0, couplings_down * under, 0.0)
+        whole = whole + jnp.where(row == ROWS - 1, couplings * over, 0.0)
+        gradient[...] = whole + rim_in[...]
+        gradient_out.start()
+
+    gradient_out = pltpu.make_async_copy(gradient, gradient_hbm, local_sem.at[11])
+    direction_out = pltpu.make_async_copy(direction, direction_hbm, local_sem.at[12])
+
+    def reduced(value, buf, me, peers, sends, recvs, beside=None):
         count = len(peers) + 1
         buf[me] = value
         copies = []
@@ -411,6 +455,8 @@
             )
             copy.start()
             copies.append(copy)
+        if beside is not None:
+            beside()
         for copy in copies:
             copy.wait()
         total = buf[0]
@@ -419,9 +465,8 @@
         return total
 
     total = jnp.sum(prods[...].T, axis=0, keepdims=True)
-    total = reduced(total, red_lev, slab, lev_peers, lev_send, lev_recv)
-    total = reduced(total, red_y, row_y, y_peers, y_send, y_recv)
-    total = reduced(total, red_z, row_z, z_peers, z_send, z_recv)
+    total = reduced(total, red_plane, row_y * slabs + slab, plane_peers, plane_send, plane_recv)
+    total = reduced(total, red_z, row_z, z_peers, z_send, z_recv, finish)
 
     spreaded = jnp.broadcast_to(total, (128, 128)).T
     of = {name: spreaded[at : at + 1, :] for name, at in slot.items()}
@@ -446,11 +491,28 @@
     def wide(value):
         return jnp.concatenate([value] * (COLS // 128), axis=1)
 
-    result = wide(-gamma) * gradient_ref[...]
+    found = wide(-gamma) * gradient[...]
     for i in range(M):
-        result = result + wide(gamma * alpha[i]) * grads[i].astype(F32)
-        result = result - wide(keep[i]) * steps[i].astype(F32)
-    direction_ref[...] = result
+        found = found + wide(gamma * alpha[i]) * pairs[M + i, :, middle]
+        found = found - wide(keep[i]) * pairs[i, :, middle]
+    direction[...] = found
+    direction_out.start()
+    gradient_out.wait()
+    direction_out.wait()
+
+
+def hand_over(first, second, first_out, second_out, staged, sem):
+    pulls = [pltpu.make_async_copy(ref, staged.at[i], sem.at[i]) for i, ref in enumerate((first, second))]
+    pushes = [
+        pltpu.make_async_copy(staged.at[i], ref, sem.at[2 + i]) for i, ref in enumerate((first_out, second_out))
+    ]
+    for copy in pulls:
+        copy.start()
+    for pull, push in zip(pulls, pushes):
+        pull.wait()
+        push.start()
+    for copy in pushes:
+        copy.wait()
 
 
 def per_device(tiles, slabs, *args):
@@ -460,11 +522,11 @@
     sems = pltpu.SemaphoreType.DMA
     nz = tiles // NY
     shape = jax.ShapeDtypeStruct((ROWS, COLS), F32)
-    return pl.pallas_call(
+    made = pl.pallas_call(
         functools.partial(kernel, tiles, slabs),
         out_shape=(shape, shape),
         in_specs=[pl.BlockSpec(memory_space=pltpu.HBM)] * 11,
-        out_specs=[pl.BlockSpec(memory_space=vmem)] * 2,
+        out_specs=[pl.BlockSpec(memory_space=pltpu.HBM)] * 2,
         scratch_shapes=[
             vmem((ROWS, FINE), F32),
             vmem((K, COLS), I32),
@@ -482,12 +544,12 @@
             vmem((OWN + FOREIGN + 1, ROWS, 128), F32),
             vmem((OWN + FOREIGN + 1, K, 128), I32),
             vmem((OWN + FOREIGN + 1, K, 128), F32),
-            vmem(((OWN + FOREIGN) * K, 128), I32),
+            vmem((OWN + FOREIGN, K, 128), I32),
             vmem((2 * EDGE // 128, K, 128), I32),
             vmem((2 * EDGE // 128, K, 128), F32),
             vmem((2 * EDGE // 128, K, 128), I32),
             vmem((2 * EDGE // 128, K, 128), F32),
-            pltpu.SMEM(((OWN + FOREIGN) * K, 128), I32),
+            pltpu.SMEM((3, K, 128), I32),
             vmem((ROWS, EXT), F32),
             vmem((2 * ROWS, EXT), BF16),
             vmem((2, COLS // WIDE, REACH, WIDE), BF16),
@@ -500,18 +562,23 @@
             vmem((2, 1, COLS), F32),
             vmem((2, 1, COLS), F32),
             vmem((ROWS, EXT), F32),
-            vmem((2, ROWS, HALO), F32),
+            vmem((ROWS, COLS), F32),
+            vmem((2 * M, ROWS, EXT), F32),
+            vmem((2 * M, COLS), F32),
+            vmem((2 * M, COLS), F32),
+            vmem((2 * M, COLS), F32),
+            vmem((2 * M, COLS), F32),
+            vmem((ROWS, COLS), F32),
+            vmem((ROWS, COLS), F32),
             vmem((128, 128), F32),
-            vmem((slabs, 1, 128), F32),
-            vmem((NY, 1, 128), F32),
+            vmem((NY * slabs, 1, 128), F32),
             vmem((nz, 1, 128), F32),
             sems((13,)),
-            sems((14,)),
-            sems((14,)),
-            sems((slabs,)),
-            sems((slabs,)),
-            sems((NY,)),
-            sems((NY,)),
+            sems((3,)),
+            sems((18,)),
+            sems((18,)),
+            sems((NY * slabs,)),
+            sems((NY * slabs,)),
             sems((nz,)),
             sems((nz,)),
         ],
@@ -520,6 +587,14 @@
         ),
         cost_estimate=pl.CostEstimate(flops=1 << 28, bytes_accessed=1 << 22, transcendentals=0),
     )(dep, off, wgt, cnt, inc, cen, vc, nbr, cpl, steps, grads)
+    return pl.pallas_call(
+        hand_over,
+        out_shape=(shape, shape),
+        in_specs=[pl.BlockSpec(memory_space=pltpu.HBM)] * 2,
+        out_specs=[pl.BlockSpec(memory_space=pltpu.HBM)] * 2,
+        scratch_shapes=[vmem((2, ROWS, COLS), F32), sems((4,))],
+        compiler_params=pltpu.CompilerParams(vmem_limit_bytes=60 * 1024 * 1024),
+    )(*made)
 
 
 def solution(mesh):

time: 45.9 us -> 37.1 us (0.81)
  the two profiles are of different devices: /device:TPU:8 before, /device:TPU:1 now
where the time goes in v3:
time: 37.1 us; the launch traced here: 37 us
  Pallas kernels  36.4 us (98%)
  between operations  0.64 us (2%)
    pallas_call x1, Pallas kernels, per_device(): pl.pallas_call(functools.partial(kernel, tiles, slabs), out_shape=(shape,...  34.8 us
    pallas_call x1, Pallas kernels, per_device(): pl.pallas_call(hand_over, out_shape=(shape, shape), in_specs=[pl.BlockSpe...  1.53 us

profile of v3, /device:TPU:1, one launch (start us, length us, event | category | flops | bytes accessed | tf_op | source)
XLA Modules:
  0.0 37.0 jit_solution(3821656223585757808)
XLA Ops:
  0.6 34.8 %shard_map.122 = (f32[16,1024]{1,0:T(8,128)}, f32[16,1024]{1,0:T(8,128)}) custom-call(f32[16,31744]{1,0:T(8,128)} %dep_hbm.1, s32[8,1024]{1,0:T(8,128)} %off_hbm.1, f32[8,1024]{1,0:T(8,128)} %wgt_hbm.1, s32[1,1024]{1,0:T(1,128)} %bitcast.1, f32[16,1024]{1,0:T(8,128)} %inc_hbm.1, f32[16,1024]{1,0:T(8,128)} %cen_hbm.1, f32[16,1024]{1,0:T(8,128)} %vc_hbm.1, ...), custom_call_target="tpu_custom_call" | custom-call | flops 268435456 | bytes 4194304 | tf_op jit(solution)/shard_map/pallas_call | solution.py:525
  35.5 1.5 %shard_map.123 = (f32[16,1024]{1,0:T(8,128)}, f32[16,1024]{1,0:T(8,128)}) custom-call(f32[16,1024]{1,0:T(8,128)} %get-tuple-element.4.first, f32[16,1024]{1,0:T(8,128)} %get-tuple-element.5.second), custom_call_target="tpu_custom_call" | custom-call | tf_op jit(solution)/shard_map/pallas_call | solution.py:590

commit v4 on v3

--- a/solution.py
+++ b/solution.py
@@ -19,7 +19,7 @@
 EDGE = 384
 OWN = COLS // 128
 FOREIGN = 5
-EARLY = 3
+EARLY = 2
 WIDE = 256
 REACH = WIDE + HALO
 NY = 4
@@ -85,7 +85,6 @@
     slots,
     inc,
     parts,
-    onehot,
     up_out,
     below,
     down_out,
@@ -107,6 +106,7 @@
     red_plane,
     red_z,
     local_sem,
+    dep_sem,
     slot_sem,
     send_sem,
     recv_sem,
@@ -154,7 +154,7 @@
         copy.start()
         return copy
 
-    loads = []
+    loads, cuts = [], []
     for i, (src, dst) in enumerate(
         [
             (off_hbm, off),
@@ -162,7 +162,6 @@
             (cnt_hbm, cnt),
             (inc_hbm, inc.at[:, HALO : HALO + COLS]),
             (vc_hbm, vc),
-            (dep_hbm, dep),
             (nbr_hbm, nbr),
             (cpl_hbm, cpl),
             (cen_hbm, cen),
@@ -173,6 +172,12 @@
         copy = pltpu.make_async_copy(src, dst, local_sem.at[i])
         copy.start()
         loads.append(copy)
+        if i == 4:
+            for g in range(8):
+                part = slice(SEG * g, min(SEG * g + SEG, FINE))
+                copy = pltpu.make_async_copy(dep_hbm.at[:, part], dep.at[:, part], dep_sem.at[g])
+                copy.start()
+                cuts.append(copy)
 
     barrier = pltpu.get_barrier_semaphore()
     greeted = plane_peers + z_peers + [spot(left, slab), spot(right, slab)]
@@ -228,7 +233,23 @@
         send(down_out, above, 7, to_lower),
     ]
 
-    loads[5].wait()
+    loads[8].wait()
+    loads[9].wait()
+    for i in range(M):
+        for at, value in ((i, steps[i]), (M + i, grads[i])):
+            field = value.astype(F32)
+            pairs[at, :, HALO : HALO + COLS] = field
+            pair_up[at : at + 1, :] = field[ROWS - 1 : ROWS]
+            pair_down[at : at + 1, :] = field[0:1]
+    pair_halos = [
+        remote(pairs.at[:, :, HALO : 2 * HALO], pairs.at[:, :, HALO + COLS : EXT], 14, to_left),
+        remote(pairs.at[:, :, COLS : COLS + HALO], pairs.at[:, :, 0:HALO], 15, to_right),
+        remote(pair_up, pair_below, 16, to_upper),
+        remote(pair_down, pair_above, 17, to_lower),
+    ]
+
+    for copy in cuts:
+        copy.wait()
     last = FINE // SEG
     tail = FINE - last * SEG
     for b in range(SEG // 128):
@@ -238,21 +259,6 @@
         else:
             pieces.append(jnp.zeros((ROWS, 128), F32))
         fine[128 * b : 128 * b + 128, :] = jnp.concatenate(pieces, axis=0).T
-
-    loads[9].wait()
-    loads[10].wait()
-    for i in range(M):
-        for at, value in ((i, steps[i]), (M + i, grads[i])):
-            field = value.astype(F32)
-            pairs[at, :, HALO : HALO + COLS] = field
-            pair_up[at : at + 1, :] = field[ROWS - 1 : ROWS]
-            pair_down[at : at + 1, :] = field[0:1]
-    halos += [
-        send(pairs.at[:, :, HALO : 2 * HALO], pairs.at[:, :, HALO + COLS : EXT], 14, to_left),
-        send(pairs.at[:, :, COLS : COLS + HALO], pairs.at[:, :, 0:HALO], 15, to_right),
-        send(pair_up, pair_below, 16, to_upper),
-        send(pair_down, pair_above, 17, to_lower),
-    ]
 
     def gather(at, rows, lanes):
         for u in lanes:
@@ -277,19 +283,6 @@
     turns = (OWN + FOREIGN - 1) // 2
 
     def pair(i, carry):
-        @pl.when(i == EARLY - 1)
-        def _():
-            for copy in lists:
-                copy.wait()
-            for at, b in enumerate((0, 1, 4, 5)):
-                f_all[OWN + at] = f_for[b]
-                w_all[OWN + at] = w_for[b]
-                r_all[OWN + at] = f_for[b] & (SEG - 1)
-            f_all[edge] = jnp.where(lane < 64, f_for[2], f_for[3])
-            w_all[edge] = jnp.where(lane < 64, w_for[2], w_for[3])
-            r_all[edge] = f_all[edge] & (SEG - 1)
-            fetch(edge, 2).start()
-
         @pl.when(i == EARLY + 2)
         def _():
             fetch(edge, 2).wait()
@@ -311,6 +304,22 @@
         later = jnp.where(i < turns - 1, block_of(i + 1), 0)
         fetch(b, 0).wait()
         gather(0, rows_a, range(128))
+
+        @pl.when(i == EARLY - 1)
+        def _():
+            for copy in lists:
+                copy.wait()
+            for copy in pair_halos:
+                copy.start()
+            for at, b in enumerate((0, 1, 4, 5)):
+                f_all[OWN + at] = f_for[b]
+                w_all[OWN + at] = w_for[b]
+                r_all[OWN + at] = f_for[b] & (SEG - 1)
+            f_all[edge] = jnp.where(lane < 64, f_for[2], f_for[3])
+            w_all[edge] = jnp.where(lane < 64, w_for[2], w_for[3])
+            r_all[edge] = f_all[edge] & (SEG - 1)
+            fetch(edge, 2).start()
+
         fetch(later, 0).start()
         result[before] = weighed(before, rows_b)
         fetch(b + 1, 1).wait()
@@ -331,14 +340,16 @@
     fetch(1, 1).wait()
     result[OWN - 1] = weighed(OWN - 1, rows_b)
 
-    for i in range(6, 9):
+    for i in range(5, 8):
         loads[i].wait()
     spots = (nbr[...] - tile * COLS + HALO) & (tiles * COLS - 1)
-    for side in range(2):
-        for b in range(COLS // WIDE):
-            where = spots[2 + side : 3 + side, WIDE * b : WIDE * b + WIDE] - (WIDE * b + HALO * side)
-            hit = lax.broadcasted_iota(I32, (REACH, WIDE), 0) == where
-            onehot[side, b] = jnp.where(hit, 1.0, 0.0).astype(BF16)
+    counted = lax.broadcasted_iota(I32, (WIDE, WIDE), 0).astype(F32).astype(BF16)
+
+    def chosen_columns(side, b, t):
+        where = spots[2 + side : 3 + side, WIDE * b : WIDE * b + WIDE] - (WIDE * (b + t) + HALO * side)
+        where = jnp.where((where >= 0) & (where < WIDE), where, -1).astype(F32)
+        hit = counted == jnp.broadcast_to(where, (ROWS, WIDE)).astype(BF16)[0:1, :]
+        return jnp.where(hit, jnp.ones((), BF16), jnp.zeros((), BF16))
 
     for copy in halos:
         copy.wait()
@@ -364,8 +375,13 @@
     for b in range(COLS // WIDE):
         total = None
         for side in range(2):
-            start = WIDE * b + HALO * side
-            got = jnp.dot(parts[:, start : start + REACH], onehot[side, b], preferred_element_type=F32)
+            got = None
+            for t in range(REACH // WIDE):
+                start = WIDE * (b + t) + HALO * side
+                found = jnp.dot(
+                    parts[:, start : start + WIDE], chosen_columns(side, b, t), preferred_element_type=F32
+                )
+                got = found if got is None else got + found
             term = cpl[2 + side : 3 + side, WIDE * b : WIDE * b + WIDE] * (got[0:ROWS] + got[ROWS : 2 * ROWS])
             total = term if total is None else total + term
         blocks.append(total)
@@ -402,16 +418,20 @@
         for side in range(2):
             start = WIDE * b + HALO * side
             carried = halves(cpl[2 + side : 3 + side, WIDE * b : WIDE * b + WIDE] * misfit[:, WIDE * b : WIDE * b + WIDE])
-            out = lax.dot_general(
-                carried, onehot[side, b], (((1,), (1,)), ((), ())), preferred_element_type=F32
-            )
-            spread[:, start : start + REACH] = spread[:, start : start + REACH] + (out[0:ROWS] + out[ROWS : 2 * ROWS])
+            for t in range(REACH // WIDE):
+                out = lax.dot_general(
+                    carried, chosen_columns(side, b, t), (((1,), (1,)), ((), ())), preferred_element_type=F32
+                )
+                at = slice(start + WIDE * t, start + WIDE * t + WIDE)
+                spread[:, at] = spread[:, at] + (out[0:ROWS] + out[ROWS : 2 * ROWS])
     rims = [
         send(spread.at[:, 0:HALO], rim_in.at[:, COLS - HALO : COLS], 12, to_left),
         send(spread.at[:, HALO + COLS : EXT], rim_in.at[:, 0:HALO], 13, to_right),
     ]
     part = mid + (cen[...] * misfit + vertical(misfit, 0.0, 0.0) + spread[:, middle])
 
+    for copy in pair_halos:
+        copy.wait()
     late = 24
     to_below = below_coupling * misfit[0:1, :]
     to_above = jnp.where(slab < slabs - 1, couplings[ROWS - 1 : ROWS, :] * misfit[ROWS - 1 : ROWS, :], 0.0)
@@ -552,7 +572,6 @@
             pltpu.SMEM((3, K, 128), I32),
             vmem((ROWS, EXT), F32),
             vmem((2 * ROWS, EXT), BF16),
-            vmem((2, COLS // WIDE, REACH, WIDE), BF16),
             vmem((2, COLS), F32),
             vmem((2, COLS), F32),
             vmem((1, COLS), F32),
@@ -574,6 +593,7 @@
             vmem((NY * slabs, 1, 128), F32),
             vmem((nz, 1, 128), F32),
             sems((13,)),
+            sems((8,)),
             sems((3,)),
             sems((18,)),
             sems((18,)),

time: 37.1 us -> 36.8 us (level)
  the two profiles are of different devices: /device:TPU:1 before, /device:TPU:8 now
where the time goes in v4:
time: 36.8 us; the launch traced here: 36.6 us
  Pallas kernels  35.9 us (98%)
  between operations  0.64 us (2%)
    pallas_call x1, Pallas kernels, per_device(): pl.pallas_call(functools.partial(kernel, tiles, slabs), out_shape=(shape,...  34.4 us
    pallas_call x1, Pallas kernels, per_device(): pl.pallas_call(hand_over, out_shape=(shape, shape), in_specs=[pl.BlockSpe...  1.53 us

profile of v4, /device:TPU:8, one launch (start us, length us, event | category | flops | bytes accessed | tf_op | source)
XLA Modules:
  0.0 36.6 jit_solution(2840540520430889717)
XLA Ops:
  0.6 34.4 %shard_map.122 = (f32[16,1024]{1,0:T(8,128)}, f32[16,1024]{1,0:T(8,128)}) custom-call(f32[16,31744]{1,0:T(8,128)} %dep_hbm.1, s32[8,1024]{1,0:T(8,128)} %off_hbm.1, f32[8,1024]{1,0:T(8,128)} %wgt_hbm.1, s32[1,1024]{1,0:T(1,128)} %bitcast.1, f32[16,1024]{1,0:T(8,128)} %inc_hbm.1, f32[16,1024]{1,0:T(8,128)} %cen_hbm.1, f32[16,1024]{1,0:T(8,128)} %vc_hbm.1, ...), custom_call_target="tpu_custom_call" | custom-call | flops 268435456 | bytes 4194304 | tf_op jit(solution)/shard_map/pallas_call | solution.py:545
  35.0 1.5 %shard_map.123 = (f32[16,1024]{1,0:T(8,128)}, f32[16,1024]{1,0:T(8,128)}) custom-call(f32[16,1024]{1,0:T(8,128)} %get-tuple-element.4.first, f32[16,1024]{1,0:T(8,128)} %get-tuple-element.5.second), custom_call_target="tpu_custom_call" | custom-call | tf_op jit(solution)/shard_map/pallas_call | solution.py:610

commit v5 on v4

--- a/solution.py
+++ b/solution.py
@@ -78,10 +78,8 @@
     f_all,
     w_all,
     r_all,
-    f_out,
-    w_out,
-    f_for,
-    w_for,
+    list_out,
+    list_in,
     slots,
     inc,
     parts,
@@ -154,6 +152,11 @@
         copy.start()
         return copy
 
+    barrier = pltpu.get_barrier_semaphore()
+    greeted = [spot(left, slab), spot(right, slab)] + plane_peers + z_peers
+    for peer in greeted:
+        pl.semaphore_signal(barrier, inc=1, device_id=peer, device_id_type=pl.DeviceIdType.MESH)
+
     loads, cuts = [], []
     for i, (src, dst) in enumerate(
         [
@@ -179,11 +182,6 @@
                 copy.start()
                 cuts.append(copy)
 
-    barrier = pltpu.get_barrier_semaphore()
-    greeted = plane_peers + z_peers + [spot(left, slab), spot(right, slab)]
-    for peer in greeted:
-        pl.semaphore_signal(barrier, inc=1, device_id=peer, device_id_type=pl.DeviceIdType.MESH)
-
     for i in range(5):
         loads[i].wait()
 
@@ -200,12 +198,12 @@
         r_all[b] = fo & (SEG - 1)
         w_all[b] = jnp.where(here, w, 0.0)
         if b < half:
-            f_out[b] = jnp.where(f < 0, f + FINE, 0)
-            w_out[b] = jnp.where(f < 0, w, 0.0)
+            list_out[b, 0:K] = jnp.where(f < 0, f + FINE, 0).astype(F32)
+            list_out[b, K : 2 * K] = jnp.where(f < 0, w, 0.0)
         if b >= OWN - half:
             at = b - OWN + 2 * half
-            f_out[at] = jnp.where(f >= FINE, f - FINE, 0)
-            w_out[at] = jnp.where(f >= FINE, w, 0.0)
+            list_out[at, 0:K] = jnp.where(f >= FINE, f - FINE, 0).astype(F32)
+            list_out[at, K : 2 * K] = jnp.where(f >= FINE, w, 0.0)
 
     def fetch(b, at):
         return pltpu.make_async_copy(r_all.at[b], slots.at[at], slot_sem.at[at])
@@ -221,10 +219,8 @@
     to_left, to_right = spot(left, slab), spot(right, slab)
     to_lower, to_upper = spot(tile, lower), spot(tile, upper)
     lists = [
-        send(f_out.at[0:half], f_for.at[0:half], 0, to_left),
-        send(w_out.at[0:half], w_for.at[0:half], 1, to_left),
-        send(f_out.at[half : 2 * half], f_for.at[half : 2 * half], 2, to_right),
-        send(w_out.at[half : 2 * half], w_for.at[half : 2 * half], 3, to_right),
+        send(list_out.at[0:half], list_in.at[0:half], 0, to_left),
+        send(list_out.at[half : 2 * half], list_in.at[half : 2 * half], 1, to_right),
     ]
     halos = [
         send(inc.at[:, HALO : 2 * HALO], inc.at[:, HALO + COLS : EXT], 4, to_left),
@@ -312,11 +308,11 @@
             for copy in pair_halos:
                 copy.start()
             for at, b in enumerate((0, 1, 4, 5)):
-                f_all[OWN + at] = f_for[b]
-                w_all[OWN + at] = w_for[b]
-                r_all[OWN + at] = f_for[b] & (SEG - 1)
-            f_all[edge] = jnp.where(lane < 64, f_for[2], f_for[3])
-            w_all[edge] = jnp.where(lane < 64, w_for[2], w_for[3])
+                f_all[OWN + at] = list_in[b, 0:K].astype(I32)
+                w_all[OWN + at] = list_in[b, K : 2 * K]
+                r_all[OWN + at] = f_all[OWN + at] & (SEG - 1)
+            f_all[edge] = jnp.where(lane < 64, list_in[2, 0:K], list_in[3, 0:K]).astype(I32)
+            w_all[edge] = jnp.where(lane < 64, list_in[2, K : 2 * K], list_in[3, K : 2 * K])
             r_all[edge] = f_all[edge] & (SEG - 1)
             fetch(edge, 2).start()
 
@@ -565,10 +561,8 @@
             vmem((OWN + FOREIGN + 1, K, 128), I32),
             vmem((OWN + FOREIGN + 1, K, 128), F32),
             vmem((OWN + FOREIGN, K, 128), I32),
-            vmem((2 * EDGE // 128, K, 128), I32),
-            vmem((2 * EDGE // 128, K, 128), F32),
-            vmem((2 * EDGE // 128, K, 128), I32),
-            vmem((2 * EDGE // 128, K, 128), F32),
+            vmem((2 * EDGE // 128, 2 * K, 128), F32),
+            vmem((2 * EDGE // 128, 2 * K, 128), F32),
             pltpu.SMEM((3, K, 128), I32),
             vmem((ROWS, EXT), F32),
             vmem((2 * ROWS, EXT), BF16),

time: 36.8 us -> 36.8 us (level)
  no operation moved by 1% of the time
where the time goes in v5:
time: 36.8 us; the launch traced here: 36.6 us
  Pallas kernels  35.9 us (98%)
  between operations  0.64 us (2%)
    pallas_call x1, Pallas kernels, per_device(): pl.pallas_call(functools.partial(kernel, tiles, slabs), out_shape=(shape,...  34.4 us
    pallas_call x1, Pallas kernels, per_device(): pl.pallas_call(hand_over, out_shape=(shape, shape), in_specs=[pl.BlockSpe...  1.53 us

profile of v5, /device:TPU:8, one launch (start us, length us, event | category | flops | bytes accessed | tf_op | source)
XLA Modules:
  0.0 36.6 jit_solution(112188656517577741)
XLA Ops:
  0.6 34.4 %shard_map.122 = (f32[16,1024]{1,0:T(8,128)}, f32[16,1024]{1,0:T(8,128)}) custom-call(f32[16,31744]{1,0:T(8,128)} %dep_hbm.1, s32[8,1024]{1,0:T(8,128)} %off_hbm.1, f32[8,1024]{1,0:T(8,128)} %wgt_hbm.1, s32[1,1024]{1,0:T(1,128)} %bitcast.1, f32[16,1024]{1,0:T(8,128)} %inc_hbm.1, f32[16,1024]{1,0:T(8,128)} %cen_hbm.1, f32[16,1024]{1,0:T(8,128)} %vc_hbm.1, ...), custom_call_target="tpu_custom_call" | custom-call | flops 268435456 | bytes 4194304 | tf_op jit(solution)/shard_map/pallas_call | solution.py:541
  35.0 1.5 %shard_map.123 = (f32[16,1024]{1,0:T(8,128)}, f32[16,1024]{1,0:T(8,128)}) custom-call(f32[16,1024]{1,0:T(8,128)} %get-tuple-element.4.first, f32[16,1024]{1,0:T(8,128)} %get-tuple-element.5.second), custom_call_target="tpu_custom_call" | custom-call | tf_op jit(solution)/shard_map/pallas_call | solution.py:604
